TPU v7x, 256 devices: a whole 4x4x8 slice. The times are simulated.
256 devices in a mesh: row: 16 (over z, y_hi), aisle: 8 (over x, y_lo), height: 2 (over core).
Axes of the slice: x: 4, y: 4 (y_hi: 2, y_lo: 2; y = y_hi * 2 + y_lo), z: 8, core: 2. Of those that a mesh axis runs over, the one named last changes fastest.
Arguments:
- probe_features: bfloat16 [128, 64, 8, 512], P('row', 'aisle', 'height'), may hold values from -8 to 8
- address_features: bfloat16 [128, 64, 8, 512], P('row', 'aisle', 'height'), may hold values from -6 to 6
- content_features: bfloat16 [128, 64, 8, 512], P('row', 'aisle', 'height'), may hold values from -6 to 6
- result_derivative: bfloat16 [128, 64, 8, 512], P('row', 'aisle', 'height'), may hold values from -6 to 6
- summary_address_table: bfloat16 [256, 512], P(('row', 'aisle', 'height')), may hold values from -8.5 to 8.5
- summary_content_table: bfloat16 [256, 512], P(('row', 'aisle', 'height')), may hold values from -6 to 6
- open_cells: int32 [128, 64, 8], P('row', 'aisle', 'height'), may hold values 0 or 1
Outputs:
- probe_derivatives: bfloat16 [128, 64, 8, 512], P('row', 'aisle', 'height')
- address_derivative: bfloat16 [128, 64, 8, 512], P('row', 'aisle', 'height')
- content_derivative: bfloat16 [128, 64, 8, 512], P('row', 'aisle', 'height')
- summary_address_derivative: float32 [256, 512], P(('row', 'aisle', 'height'))
- summary_content_derivative: float32 [256, 512], P(('row', 'aisle', 'height'))
Inputs may be any that keep to these rules, and one draw needn't show every extreme that they name: `open_cells`: 1 marks a fluid token, 0 a solid one.
All inputs are finite; a program needn't handle non-finite values. No bound on the sum of `open_cells` on one device may be relied on, other than what follows from the above.
Results may differ from a plain program's by a relative error of at most 0.012.
The roundings to bfloat16 on the way count: a program that leaves them out, or rounds other values in their place, can miss the bound.
Values may be sent and summed in bfloat16 or wider, within the bound.
No kernel may reach another device: no remote copies, remote signals or barrier semaphores. Data moves between devices by JAX's collectives and lax.ppermute only.
A program may use at most 128 MiB of HBM per device.

v0:
```python
import jax
import jax.numpy as jnp
from jax import lax
from jax.sharding import PartitionSpec as P

NUM_ATTN_BRANCH = 8
REACH = 3


NEGATIVE = -1e30


def padded(cells, sides, width):
    for axis, dim in sides:
        count = lax.axis_size(axis)
        head = lax.slice_in_dim(cells, 0, width, axis=dim)
        tail = lax.slice_in_dim(cells, cells.shape[dim] - width, cells.shape[dim], axis=dim)
        cells = jnp.concatenate(
            [
                lax.ppermute(tail, axis, [(i, (i + 1) % count) for i in range(count)]),
                cells,
                lax.ppermute(head, axis, [((i + 1) % count, i) for i in range(count)]),
            ],
            axis=dim,
        )
    return cells


def grid_codes(extent_row, extent_wide, extent_tall):
    positions = jnp.arange(extent_row * extent_wide * extent_tall, dtype=jnp.int32)
    return (
        positions // (extent_wide * extent_tall),
        positions // extent_tall % extent_wide,
        positions % extent_tall,
    )


def near_table(extent_row, extent_wide, extent_tall):
    inner_row, inner_wide, inner_tall = grid_codes(extent_row, extent_wide, extent_tall)
    slab_row, slab_wide, slab_tall = grid_codes(
        extent_row + 2 * REACH, extent_wide + 2 * REACH, extent_tall + 2 * REACH
    )
    close_row = jnp.abs(inner_row[:, None] + REACH - slab_row[None, :]) <= REACH
    close_wide = jnp.abs(inner_wide[:, None] + REACH - slab_wide[None, :]) <= REACH
    close_tall = jnp.abs(inner_tall[:, None] + REACH - slab_tall[None, :]) <= REACH
    return close_row & close_wide & close_tall


def inside_grid(extent_wide, extent_tall):
    spot_wide = (
        lax.axis_index("aisle") * extent_wide
        - REACH
        + jnp.arange(extent_wide + 2 * REACH, dtype=jnp.int32)
    )
    spot_tall = (
        lax.axis_index("height") * extent_tall
        - REACH
        + jnp.arange(extent_tall + 2 * REACH, dtype=jnp.int32)
    )
    good_wide = (spot_wide >= 0) & (spot_wide < extent_wide * lax.axis_size("aisle"))
    good_tall = (spot_tall >= 0) & (spot_tall < extent_tall * lax.axis_size("height"))
    return good_wide[:, None] & good_tall[None, :]


def head_cols(matrix, attention_branch_batch, heads_now, level_reach_along):
    piece = lax.dynamic_slice_in_dim(
        matrix,
        attention_branch_batch * heads_now * level_reach_along,
        heads_now * level_reach_along,
        1,
    )
    return piece.reshape(matrix.shape[0], heads_now, level_reach_along)


def appended_slots(target, piece, col_start):
    flat_piece = piece.reshape(piece.shape[0], -1)
    location = (jnp.int32(0), col_start)
    current = lax.dynamic_slice(target, location, flat_piece.shape)
    return lax.dynamic_update_slice(target, current + flat_piece, location)


def fold_axis(field, along, cells):
    middle = lax.slice_in_dim(field, 2 * REACH, 2 * REACH + cells, axis=along)
    lower = lax.slice_in_dim(field, 0, REACH, axis=along)
    upper = lax.slice_in_dim(field, cells + 3 * REACH, cells + 4 * REACH, axis=along)
    spread_low = [(0, 0)] * field.ndim
    spread_low[along] = (0, cells - REACH)
    spread_high = [(0, 0)] * field.ndim
    spread_high[along] = (cells - REACH, 0)
    return middle + jnp.pad(lower, spread_low) + jnp.pad(upper, spread_high)


def query_pass(
    asker_component,
    upstream_derivative,
    key_section,
    value_section,
    digest_locator_lines_of,
    summary_content_rows,
    permitted_mask,
    sharpness_multiplier,
):
    affinity_component = (
        jnp.einsum("qnd,knd->nqk", asker_component, key_section, preferred_element_type=jnp.float32)
        * sharpness_multiplier
    )
    affinity_component = jnp.where(permitted_mask[None], affinity_component, NEGATIVE)
    digest_affinity = (
        jnp.einsum(
            "gvf,wvf->vgw",
            asker_component,
            digest_locator_lines_of,
            preferred_element_type=jnp.float32,
        )
        * sharpness_multiplier
    )
    ceiling_bound = jnp.maximum(
        jnp.max(affinity_component, axis=-1), jnp.max(digest_affinity, axis=-1)
    )
    exponentiated_scores = jnp.exp(affinity_component - ceiling_bound[..., None])
    summary_exps = jnp.exp(digest_affinity - ceiling_bound[..., None])
    overall_accum = jnp.sum(exponentiated_scores, axis=-1) + jnp.sum(summary_exps, axis=-1)
    attend = exponentiated_scores / overall_accum[..., None]
    summary_probabilities = summary_exps / overall_accum[..., None]
    attend_low = attend.astype(jnp.bfloat16)
    summary_bias = summary_probabilities.astype(jnp.bfloat16)
    output = jnp.einsum(
        "nqk,knd->qnd", attend_low, value_section, preferred_element_type=jnp.float32
    )
    output = output + jnp.einsum(
        "xsj,jxi->sxi", summary_bias, summary_content_rows, preferred_element_type=jnp.float32
    )
    result_inner_product = jnp.einsum(
        "qnd,qnd->nq", upstream_derivative.astype(jnp.float32), output
    )
    attend_grad = jnp.einsum(
        "qnd,knd->nqk", upstream_derivative, value_section, preferred_element_type=jnp.float32
    )
    summary_derivative = jnp.einsum(
        "gvf,wvf->vgw",
        upstream_derivative,
        summary_content_rows,
        preferred_element_type=jnp.float32,
    )
    score_grad = (attend * (attend_grad - result_inner_product[..., None])).astype(jnp.bfloat16)
    digest_affinity_change = (
        summary_probabilities * (summary_derivative - result_inner_product[..., None])
    ).astype(jnp.bfloat16)
    asker_change = jnp.einsum(
        "nqk,knd->qnd", score_grad, key_section, preferred_element_type=jnp.float32
    )
    asker_change = asker_change + jnp.einsum(
        "xsj,jxi->sxi",
        digest_affinity_change,
        digest_locator_lines_of,
        preferred_element_type=jnp.float32,
    )
    summary_address_sensitivity = (
        jnp.einsum(
            "noj,one->jne",
            digest_affinity_change,
            asker_component,
            preferred_element_type=jnp.float32,
        )
        * sharpness_multiplier
    )
    summary_content_sensitivity = jnp.einsum(
        "noj,one->jne", summary_bias, upstream_derivative, preferred_element_type=jnp.float32
    )
    log_total = ceiling_bound + jnp.log(overall_accum)
    return (
        asker_change * sharpness_multiplier,
        summary_address_sensitivity,
        summary_content_sensitivity,
        score_grad,
        attend_low,
        log_total,
        result_inner_product,
    )


def per_device(
    probe_features,
    address_features,
    content_features,
    result_derivative,
    summary_address_table,
    summary_content_table,
    open_cells,
):
    extent_row, extent_wide, extent_tall, broad_span = probe_features.shape
    heads_now = min(2, NUM_ATTN_BRANCH)
    level_reach_along = broad_span // NUM_ATTN_BRANCH
    groups = NUM_ATTN_BRANCH // heads_now
    neighbour_radius = heads_now * level_reach_along
    sharpness_multiplier = float(level_reach_along) ** (-0.5)
    side = 4
    row_blocks = extent_row // side
    wide_blocks = extent_wide // side
    inner_dims = (side, side, extent_tall)
    inner = side * side * extent_tall
    slab_dims = (side + 2 * REACH, side + 2 * REACH, extent_tall + 2 * REACH)
    slab_cells = slab_dims[0] * slab_dims[1] * slab_dims[2]
    padded_cells = (slab_cells + 127) // 128 * 128
    extra_cells = padded_cells - slab_cells
    zero = jnp.int32(0)
    wider_keys, wider_values, wider_fluid = (
        padded(address_features, (("row", 0), ("aisle", 1), ("height", 2)), REACH),
        padded(content_features, (("row", 0), ("aisle", 1), ("height", 2)), REACH),
        padded(open_cells.astype(jnp.bfloat16), (("row", 0), ("aisle", 1), ("height", 2)), REACH),
    )
    in_grid = inside_grid(extent_wide, extent_tall)
    usable = (wider_fluid > 0.5) & in_grid[None]
    joined_addresses, every_values = (
        lax.all_gather(summary_address_table, ("row", "aisle", "height"), axis=0, tiled=True),
        lax.all_gather(summary_content_table, ("row", "aisle", "height"), axis=0, tiled=True),
    )
    summary_tokens_list = joined_addresses.shape[0]
    near = jnp.pad(near_table(side, side, extent_tall), ((0, 0), (0, extra_cells)))

    def cut_slab(field, row_start, wide_start, attention_branch_batch):
        piece = lax.dynamic_slice(
            field,
            (row_start, wide_start, zero, attention_branch_batch * neighbour_radius),
            slab_dims + (neighbour_radius,),
        )
        flat = jnp.pad(piece.reshape(slab_cells, neighbour_radius), ((0, extra_cells), (0, 0)))
        return flat.reshape(padded_cells, heads_now, level_reach_along)

    def cut_inner(field, row_start, wide_start, attention_branch_batch):
        piece = lax.dynamic_slice(
            field,
            (row_start, wide_start, zero, attention_branch_batch * neighbour_radius),
            inner_dims + (neighbour_radius,),
        )
        return piece.reshape(inner, heads_now, level_reach_along)

    def cut_mask(field, row_start, wide_start):
        piece = lax.dynamic_slice(field, (row_start, wide_start, zero), slab_dims)
        return jnp.pad(piece.reshape(slab_cells), (0, extra_cells))

    def query_step(row_start, wide_start, attention_branch_batch):
        asker_component = cut_inner(probe_features, row_start, wide_start, attention_branch_batch)
        upstream_derivative = cut_inner(
            result_derivative, row_start, wide_start, attention_branch_batch
        )
        key_section = cut_slab(wider_keys, row_start, wide_start, attention_branch_batch)
        value_section = cut_slab(wider_values, row_start, wide_start, attention_branch_batch)
        permitted_mask = near & cut_mask(usable, row_start, wide_start)[None, :]
        parts = query_pass(
            asker_component,
            upstream_derivative,
            key_section,
            value_section,
            head_cols(joined_addresses, attention_branch_batch, heads_now, level_reach_along),
            head_cols(every_values, attention_branch_batch, heads_now, level_reach_along),
            permitted_mask,
            sharpness_multiplier,
        )
        return (asker_component, upstream_derivative, parts)

    def put_inner(target, piece, row_start, wide_start, col_start):
        shaped = piece.reshape(inner_dims + (piece.shape[-2] * piece.shape[-1],)).astype(
            target.dtype
        )
        return lax.dynamic_update_slice(target, shaped, (row_start, wide_start, zero, col_start))

    grid_shape = (extent_row, extent_wide, extent_tall, broad_span)
    probe_sensitivity = jnp.zeros(grid_shape, jnp.bfloat16)
    digest_locator_sums = jnp.zeros((summary_tokens_list, broad_span), jnp.float32)
    summary_content_accum = jnp.zeros((summary_tokens_list, broad_span), jnp.float32)
    address_sensitivity = jnp.zeros(grid_shape, jnp.bfloat16)
    content_sensitivity = jnp.zeros(grid_shape, jnp.bfloat16)
    rim_shape = (
        extent_row + 2 * REACH,
        extent_wide + 2 * REACH,
        extent_tall + 2 * REACH,
        neighbour_radius,
    )
    piece_shape = slab_dims + (neighbour_radius,)

    def group_turn(attention_branch_batch, running_state):
        (
            probe_sensitivity,
            address_sensitivity,
            content_sensitivity,
            digest_locator_sums,
            summary_content_accum,
        ) = running_state

        def block_turn(index, interior_state):
            (
                probe_sensitivity,
                address_margin,
                content_margin,
                digest_locator_sums,
                summary_content_accum,
            ) = interior_state
            row_start = index * side
            for wide_index in range(wide_blocks):
                wide_start = jnp.int32(wide_index * side)
                asker_component, upstream_derivative, parts = query_step(
                    row_start, wide_start, attention_branch_batch
                )
                (
                    asker_change,
                    summary_address_sensitivity,
                    summary_content_sensitivity,
                    score_grad,
                    attend_low,
                    log_total,
                    result_inner_product,
                ) = parts
                slab_key = (
                    jnp.einsum(
                        "nqk,qnd->knd",
                        score_grad,
                        asker_component,
                        preferred_element_type=jnp.float32,
                    )
                    * sharpness_multiplier
                )
                slab_value = jnp.einsum(
                    "nqk,qnd->knd",
                    attend_low,
                    upstream_derivative,
                    preferred_element_type=jnp.float32,
                )
                slab_key = slab_key[:slab_cells].reshape(piece_shape)
                slab_value = slab_value[:slab_cells].reshape(piece_shape)
                location = (row_start, wide_start, zero, zero)
                address_margin = lax.dynamic_update_slice(
                    address_margin,
                    lax.dynamic_slice(address_margin, location, piece_shape) + slab_key,
                    location,
                )
                content_margin = lax.dynamic_update_slice(
                    content_margin,
                    lax.dynamic_slice(content_margin, location, piece_shape) + slab_value,
                    location,
                )
                probe_sensitivity = put_inner(
                    probe_sensitivity,
                    asker_change,
                    row_start,
                    wide_start,
                    attention_branch_batch * neighbour_radius,
                )
                digest_locator_sums = appended_slots(
                    digest_locator_sums,
                    summary_address_sensitivity,
                    attention_branch_batch * neighbour_radius,
                )
                summary_content_accum = appended_slots(
                    summary_content_accum,
                    summary_content_sensitivity,
                    attention_branch_batch * neighbour_radius,
                )
            return (
                probe_sensitivity,
                address_margin,
                content_margin,
                digest_locator_sums,
                summary_content_accum,
            )

        start_rims = (
            probe_sensitivity,
            jnp.zeros(rim_shape, jnp.float32),
            jnp.zeros(rim_shape, jnp.float32),
            digest_locator_sums,
            summary_content_accum,
        )
        (
            probe_sensitivity,
            address_margin,
            content_margin,
            digest_locator_sums,
            summary_content_accum,
        ) = lax.fori_loop(0, row_blocks, block_turn, start_rims)
        folded_keys, folded_values = (
            padded(address_margin, (("row", 0), ("aisle", 1), ("height", 2)), REACH),
            padded(content_margin, (("row", 0), ("aisle", 1), ("height", 2)), REACH),
        )
        for along, cells in ((0, extent_row), (1, extent_wide), (2, extent_tall)):
            folded_keys = fold_axis(folded_keys, along, cells)
            folded_values = fold_axis(folded_values, along, cells)
        corner = (zero, zero, zero, attention_branch_batch * neighbour_radius)
        address_sensitivity = lax.dynamic_update_slice(
            address_sensitivity, folded_keys.astype(jnp.bfloat16), corner
        )
        content_sensitivity = lax.dynamic_update_slice(
            content_sensitivity, folded_values.astype(jnp.bfloat16), corner
        )
        return (
            probe_sensitivity,
            address_sensitivity,
            content_sensitivity,
            digest_locator_sums,
            summary_content_accum,
        )

    initial_state = (
        probe_sensitivity,
        address_sensitivity,
        content_sensitivity,
        digest_locator_sums,
        summary_content_accum,
    )
    (
        probe_sensitivity,
        address_sensitivity,
        content_sensitivity,
        digest_locator_sums,
        summary_content_accum,
    ) = lax.fori_loop(0, groups, group_turn, initial_state)
    summary_address_derivative, summary_content_derivative = (
        lax.psum_scatter(
            digest_locator_sums, ("row", "aisle", "height"), scatter_dimension=0, tiled=True
        ),
        lax.psum_scatter(
            summary_content_accum, ("row", "aisle", "height"), scatter_dimension=0, tiled=True
        ),
    )
    return (
        probe_sensitivity,
        address_sensitivity,
        content_sensitivity,
        summary_address_derivative,
        summary_content_derivative,
    )


def solution(mesh):
    in_specs = (
        P("row", "aisle", "height", None),
        P("row", "aisle", "height", None),
        P("row", "aisle", "height", None),
        P("row", "aisle", "height", None),
        P(("row", "aisle", "height"), None),
        P(("row", "aisle", "height"), None),
        P("row", "aisle", "height"),
    )
    out_specs = (
        P("row", "aisle", "height", None),
        P("row", "aisle", "height", None),
        P("row", "aisle", "height", None),
        P(("row", "aisle", "height"), None),
        P(("row", "aisle", "height"), None),
    )
    return jax.shard_map(
        per_device, mesh=mesh, in_specs=in_specs, out_specs=out_specs, check_vma=False
    )
```

profile of v0, /device:TPU:1, one launch (start us, length us, event | category | flops | bytes accessed | tf_op | source)
XLA Modules:
  0.0 2185.2 jit_solution(1293666796845631336)
XLA Ops:
  8.1 3.8 collective-permute-start.18
  11.9 5.4 collective-permute-start.19
  18.4 5.1 collective-permute-start.25
  25.0 345.1 %all-gather = bf16[256,1,512]{2,1,0:T(2,128)(2,1)S(1)} all-gather(bf16[1,1,512]{2,1,0:T(2,128)(2,1)} %bitcast.292), channel_id=1, replica_groups=mesh['row'=16,'aisle'=8,'height'=2] {'row','aisle','height'}, dimensions={0}, use_global_device_ids=true | all-gather | bytes 263168 | tf_op jit(solution)/shard_map/all_gather | solution.py:215
  370.3 3.6 collective-permute-start.21
  375.1 4.3 collective-permute-start.13
  381.6 3.8 collective-permute-start.27
  385.8 5.4 collective-permute-done.26
  391.1 3.8 collective-permute-done.27
  396.8 6.7 collective-permute-start.28
  406.6 340.8 %all-gather.1 = bf16[256,1,512]{2,1,0:T(2,128)(2,1)S(1)} all-gather(bf16[1,1,512]{2,1,0:T(2,128)(2,1)S(1)} %bitcast.293), channel_id=1, replica_groups=mesh['row'=16,'aisle'=8,'height'=2] {'row','aisle','height'}, dimensions={0}, use_global_device_ids=true | all-gather | bytes 263168 | tf_op jit(solution)/shard_map/all_gather | solution.py:216
  752.0 3.1 copy.154
  757.1 3.2 copy.152
  764.3 1157.8 %while.79 = (s32[]{:T(128)}, bf16[8,8,4,512]{3,2,1,0:T(4,128)(2,1)}, bf16[8,8,4,512]{3,2,1,0:T(4,128)(2,1)}, bf16[8,8,4,512]{3,2,1,0:T(4,128)(2,1)}, f32[256,512...) while((s32[]{:T(128)}, ...), condition=%wide.region_11.12_spmd, body=%wide.region_0.11_spmd.sunk | while | flops 275074304 | bytes 163826192 | solution.py:416
  765.6 214.2 %while.80 = (s32[]{:T(128)}, bf16[8,8,4,512]{3,2,1,0:T(4,128)(2,1)}, f32[14,14,10,128]{3,2,1,0:T(8,128)S(1)}, f32[14,14,10,128]{3,2,1,0:T(8,128)S(1)}, f32[256,5...) while((s32[]{:T(128)}, ...), condition=%wide.region_10.10_spmd, body=%wide.region_1.9_spmd.sunk | while | flops 258051328 | bytes 62362132 | solution.py:380
  839.8 2.8 reshape.509
  980.3 5.1 collective-permute-start.7
  985.8 5.1 collective-permute-start.1
  991.6 8.1 collective-permute-done.7
  1002.0 11.8 collective-permute-done.1
  1018.5 9.1 collective-permute-done.9
  1029.0 4.0 collective-permute-start.10
  1033.1 2.9 collective-permute-done.2
  1050.1 214.2 %while.80 = (s32[]{:T(128)}, bf16[8,8,4,512]{3,2,1,0:T(4,128)(2,1)}, f32[14,14,10,128]{3,2,1,0:T(8,128)S(1)}, f32[14,14,10,128]{3,2,1,0:T(8,128)S(1)}, f32[256,5...) while((s32[]{:T(128)}, ...), condition=%wide.region_10.10_spmd, body=%wide.region_1.9_spmd.sunk | while | flops 258051328 | bytes 62362132 | solution.py:380
  1264.6 5.0 collective-permute-start.6
  1270.1 2.9 collective-permute-start
  1275.3 9.9 collective-permute-done.6
  1288.5 19.3 collective-permute-done
  1311.3 5.5 collective-permute-done.9
  1320.3 8.5 collective-permute-done.2
  1342.1 214.1 %while.80 = (s32[]{:T(128)}, bf16[8,8,4,512]{3,2,1,0:T(4,128)(2,1)}, f32[14,14,10,128]{3,2,1,0:T(8,128)S(1)}, f32[14,14,10,128]{3,2,1,0:T(8,128)S(1)}, f32[256,5...) while((s32[]{:T(128)}, ...), condition=%wide.region_10.10_spmd, body=%wide.region_1.9_spmd.sunk | while | flops 258051328 | bytes 62362132 | solution.py:380
  1562.5 4.7 collective-permute-start.1
  1567.2 7.4 collective-permute-done.6
  1575.0 3.7 collective-permute-done.7
  1580.4 12.5 collective-permute-done
  1593.3 8.2 collective-permute-done.1
  1603.2 3.0 collective-permute-done.9
  1609.8 11.2 collective-permute-done.2
  1634.1 214.1 %while.80 = (s32[]{:T(128)}, bf16[8,8,4,512]{3,2,1,0:T(4,128)(2,1)}, f32[14,14,10,128]{3,2,1,0:T(8,128)S(1)}, f32[14,14,10,128]{3,2,1,0:T(8,128)S(1)}, f32[256,5...) while((s32[]{:T(128)}, ...), condition=%wide.region_10.10_spmd, body=%wide.region_1.9_spmd.sunk | while | flops 258051328 | bytes 62362132 | solution.py:380
  1848.6 5.1 collective-permute-start.7
  1854.1 5.1 collective-permute-start.1
  1859.2 5.4 collective-permute-done.6
  1865.0 2.9 collective-permute-done.7
  1869.6 13.4 collective-permute-done
  1883.4 7.3 collective-permute-done.1
  1892.4 3.8 collective-permute-done.9
  1898.7 10.1 collective-permute-done.2
  1926.3 249.3 %all-reduce.18.cloned.1.call-done = (f32[256,512]{1,0:T(8,128)}, f32[256,512]{1,0:T(8,128)}) async-done(((f32[256,512]{1,0:T(8,128)}, f32[256,512]{1,0:T(8,128)}), (f32[256,512]{1,0:T(8,128)}, f32[256,512]{1,0:T(8,128)})) %all-reduce.18.cloned.1.call-update) | async-done | bytes 1048592
  (1626 shorter events, 979.0 us)
Async XLA Ops:
  7.2 2168.4 %all-reduce.18.cloned.1.call-start = ((), (), s32[]{:S(2)}) async-start(), calls=%async_computation | async-start | bytes 2097152
  8.1 362.0 %collective-permute-start.18 = (bf16[3,8,4]{0,1,2:T(8,128)(2,1)S(1)}, bf16[3,8,4]{0,1,2:T(8,128)(2,1)S(1)}, u32[]{:S(2)}, u32[]{:S(2)}) collective-permute-start(bf16[3,8,4]{0,1,2:T(8,128)(2,1)S(1)} %get-tuple-element.1003), channel_id=1, source_target_pairs={{0,16},{16,32},{32,48},{48,64},{64,80},{80,96},{96,112},{112,128},... | collective-permute-start | bytes 584 | tf_op jit(solution)/shard_map/ppermute | solution.py:20
  11.9 358.3 %collective-permute-start.19 = (bf16[3,8,4]{0,1,2:T(8,128)(2,1)S(1)}, bf16[3,8,4]{0,1,2:T(8,128)(2,1)S(1)}, u32[]{:S(2)}, u32[]{:S(2)}) collective-permute-start(bf16[3,8,4]{0,1,2:T(8,128)(2,1)S(1)} %get-tuple-element.1004), channel_id=1, source_target_pairs={{16,0},{32,16},{48,32},{64,48},{80,64},{96,80},{112,96},{128,112},... | collective-permute-start | bytes 584 | tf_op jit(solution)/shard_map/ppermute | solution.py:22
  18.3 362.7 %collective-permute-start.24 = (bf16[3,8,4,512]{3,1,2,0:T(8,128)(2,1)S(1)}, bf16[3,8,4,512]{3,1,2,0:T(8,128)(2,1)S(1)}, u32[]{:S(2)}, u32[]{:S(2)}) collective-permute-start(bf16[3,8,4,512]{3,1,2,0:T(8,128)(2,1)S(1)} %copy.191), channel_id=1, source_target_pairs={{0,16},{16,32},{32,48},{48,64},{64,80},{80,96},{96,112},{112,128},... | collective-permute-start | bytes 294920 | tf_op jit(solution)/shard_map/ppermute | solution.py:20
  18.4 362.8 %collective-permute-start.25 = (bf16[3,8,4,512]{3,1,2,0:T(8,128)(2,1)S(1)}, bf16[3,8,4,512]{3,1,2,0:T(8,128)(2,1)S(1)}, u32[]{:S(2)}, u32[]{:S(2)}) collective-permute-start(bf16[3,8,4,512]{3,1,2,0:T(8,128)(2,1)S(1)} %copy.192), channel_id=1, source_target_pairs={{16,0},{32,16},{48,32},{64,48},{80,64},{96,80},{112,96},{128,112},... | collective-permute-start | bytes 294920 | tf_op jit(solution)/shard_map/ppermute | solution.py:22
  379.6 26.9 %collective-permute-start.22 = (bf16[14,14,3]{1,0,2:T(8,128)(2,1)S(1)}, bf16[14,14,3]{1,0,2:T(8,128)(2,1)S(1)}, u32[]{:S(2)}, u32[]{:S(2)}) collective-permute-start(bf16[14,14,3]{1,0,2:T(8,128)(2,1)S(1)} %get-tuple-element.999), channel_id=1, source_target_pairs={{0,1},{1,0},{2,3},{3,2},{4,5},{5,4},{6,7},{7,6},{8,9},{9,8},{10,11... | collective-permute-start | bytes 3536 | tf_op jit(solution)/shard_map/ppermute | solution.py:20
  381.1 368.0 %collective-permute-start.23 = (bf16[14,14,3]{1,0,2:T(8,128)(2,1)S(1)}, bf16[14,14,3]{1,0,2:T(8,128)(2,1)S(1)}, u32[]{:S(2)}, u32[]{:S(2)}) collective-permute-start(bf16[14,14,3]{1,0,2:T(8,128)(2,1)S(1)} %get-tuple-element.1000), channel_id=1, source_target_pairs={{1,0},{0,1},{3,2},{2,3},{5,4},{4,5},{7,6},{6,7},{9,8},{8,9},{11,10... | collective-permute-start | bytes 3536 | tf_op jit(solution)/shard_map/ppermute | solution.py:22
  385.7 17.8 collective-permute-start.14
  396.8 353.2 %collective-permute-start.28 = (bf16[14,14,3,512]{3,1,2,0:T(8,128)(2,1)}, bf16[14,14,3,512]{3,1,2,0:T(8,128)(2,1)}, u32[]{:S(2)}, u32[]{:S(2)}) collective-permute-start(bf16[14,14,3,512]{3,1,2,0:T(8,128)(2,1)} %get-tuple-element.987), channel_id=1, source_target_pairs={{0,1},{1,0},{2,3},{3,2},{4,5},{5,4},{6,7},{7,6},{8,9},{9,8},{10,11... | collective-permute-start | bytes 1806344 | tf_op jit(solution)/shard_map/ppermute | solution.py:20
  403.5 346.5 %collective-permute-start.29 = (bf16[14,14,3,512]{3,1,2,0:T(8,128)(2,1)}, bf16[14,14,3,512]{3,1,2,0:T(8,128)(2,1)}, u32[]{:S(2)}, u32[]{:S(2)}) collective-permute-start(bf16[14,14,3,512]{3,1,2,0:T(8,128)(2,1)} %get-tuple-element.988), channel_id=1, source_target_pairs={{1,0},{0,1},{3,2},{2,3},{5,4},{4,5},{7,6},{6,7},{9,8},{8,9},{11,10... | collective-permute-start | bytes 1806344 | tf_op jit(solution)/shard_map/ppermute | solution.py:22
  405.4 349.7 %collective-permute-start.16 = (bf16[14,14,3,512]{3,1,2,0:T(8,128)(2,1)}, bf16[14,14,3,512]{3,1,2,0:T(8,128)(2,1)}, u32[]{:S(2)}, u32[]{:S(2)}) collective-permute-start(bf16[14,14,3,512]{3,1,2,0:T(8,128)(2,1)} %get-tuple-element.989), channel_id=1, source_target_pairs={{0,1},{1,0},{2,3},{3,2},{4,5},{5,4},{6,7},{7,6},{8,9},{9,8},{10,11... | collective-permute-start | bytes 1806344 | tf_op jit(solution)/shard_map/ppermute | solution.py:20
  406.5 348.6 %collective-permute-start.17 = (bf16[14,14,3,512]{3,1,2,0:T(8,128)(2,1)}, bf16[14,14,3,512]{3,1,2,0:T(8,128)(2,1)}, u32[]{:S(2)}, u32[]{:S(2)}) collective-permute-start(bf16[14,14,3,512]{3,1,2,0:T(8,128)(2,1)} %get-tuple-element.990), channel_id=1, source_target_pairs={{1,0},{0,1},{3,2},{2,3},{5,4},{4,5},{7,6},{6,7},{9,8},{8,9},{11,10... | collective-permute-start | bytes 1806344 | tf_op jit(solution)/shard_map/ppermute | solution.py:22
  980.3 19.5 collective-permute-start.7
  985.7 16.0 collective-permute-start
  985.8 28.0 %collective-permute-start.1 = (f32[3,14,10,128]{3,1,2,0:T(8,128)S(1)}, f32[3,14,10,128]{3,1,2,0:T(8,128)S(1)}, u32[]{:S(2)}, u32[]{:S(2)}) collective-permute-start(f32[3,14,10,128]{3,1,2,0:T(8,128)S(1)} %get-tuple-element.1255), channel_id=1, source_target_pairs={{16,0},{32,16},{48,32},{64,48},{80,64},{96,80},{112,96},{128,112},... | collective-permute-start | bytes 645128 | tf_op jit(solution)/shard_map/while/body/eval_jaxpr/ppermute | solution.py:22
  999.9 18.5 collective-permute-start.8
  1000.0 27.5 %collective-permute-start.9 = (f32[20,3,10,128]{3,1,2,0:T(4,128)S(1)}, f32[20,3,10,128]{3,1,2,0:T(4,128)S(1)}, u32[]{:S(2)}, u32[]{:S(2)}) collective-permute-start(f32[20,3,10,128]{3,1,2,0:T(4,128)S(1)} %get-tuple-element.1263), channel_id=1, source_target_pairs={{0,2},{2,4},{4,6},{6,8},{8,10},{10,12},{12,14},{14,0},{1,3},{3,5},... | collective-permute-start | bytes 921608 | tf_op jit(solution)/shard_map/while/body/eval_jaxpr/ppermute | solution.py:20
  1014.0 22.0 %collective-permute-start.2 = (f32[20,3,10,128]{3,1,2,0:T(4,128)S(1)}, f32[20,3,10,128]{3,1,2,0:T(4,128)S(1)}, u32[]{:S(2)}, u32[]{:S(2)}) collective-permute-start(f32[20,3,10,128]{3,1,2,0:T(4,128)S(1)} %get-tuple-element.1256), channel_id=1, source_target_pairs={{2,0},{4,2},{6,4},{8,6},{10,8},{12,10},{14,12},{0,14},{3,1},{5,3},... | collective-permute-start | bytes 921608 | tf_op jit(solution)/shard_map/while/body/eval_jaxpr/ppermute | solution.py:22
  1014.1 22.3 %collective-permute-start.3 = (f32[20,3,10,128]{3,1,2,0:T(4,128)S(1)}, f32[20,3,10,128]{3,1,2,0:T(4,128)S(1)}, u32[]{:S(2)}, u32[]{:S(2)}) collective-permute-start(f32[20,3,10,128]{3,1,2,0:T(4,128)S(1)} %get-tuple-element.1257), channel_id=1, source_target_pairs={{0,2},{2,4},{4,6},{6,8},{8,10},{10,12},{12,14},{14,0},{1,3},{3,5},... | collective-permute-start | bytes 921608 | tf_op jit(solution)/shard_map/while/body/eval_jaxpr/ppermute | solution.py:20
  1264.6 20.5 collective-permute-start.6
  1269.6 17.1 collective-permute-start.7
  1270.1 37.7 %collective-permute-start = (f32[3,14,10,128]{3,1,2,0:T(8,128)S(1)}, f32[3,14,10,128]{3,1,2,0:T(8,128)S(1)}, u32[]{:S(2)}, u32[]{:S(2)}) collective-permute-start(f32[3,14,10,128]{3,1,2,0:T(8,128)S(1)} %get-tuple-element.1254), channel_id=1, source_target_pairs={{0,16},{16,32},{32,48},{48,64},{64,80},{80,96},{96,112},{112,128},... | collective-permute-start | bytes 645128 | tf_op jit(solution)/shard_map/while/body/eval_jaxpr/ppermute | solution.py:20
  1273.0 36.5 %collective-permute-start.1 = (f32[3,14,10,128]{3,1,2,0:T(8,128)S(1)}, f32[3,14,10,128]{3,1,2,0:T(8,128)S(1)}, u32[]{:S(2)}, u32[]{:S(2)}) collective-permute-start(f32[3,14,10,128]{3,1,2,0:T(8,128)S(1)} %get-tuple-element.1255), channel_id=1, source_target_pairs={{16,0},{32,16},{48,32},{64,48},{80,64},{96,80},{112,96},{128,112},... | collective-permute-start | bytes 645128 | tf_op jit(solution)/shard_map/while/body/eval_jaxpr/ppermute | solution.py:22
  1286.9 24.4 %collective-permute-start.8 = (f32[20,3,10,128]{3,1,2,0:T(4,128)S(1)}, f32[20,3,10,128]{3,1,2,0:T(4,128)S(1)}, u32[]{:S(2)}, u32[]{:S(2)}) collective-permute-start(f32[20,3,10,128]{3,1,2,0:T(4,128)S(1)} %get-tuple-element.1262), channel_id=1, source_target_pairs={{2,0},{4,2},{6,4},{8,6},{10,8},{12,10},{14,12},{0,14},{3,1},{5,3},... | collective-permute-start | bytes 921608 | tf_op jit(solution)/shard_map/while/body/eval_jaxpr/ppermute | solution.py:22
  1287.0 29.8 %collective-permute-start.9 = (f32[20,3,10,128]{3,1,2,0:T(4,128)S(1)}, f32[20,3,10,128]{3,1,2,0:T(4,128)S(1)}, u32[]{:S(2)}, u32[]{:S(2)}) collective-permute-start(f32[20,3,10,128]{3,1,2,0:T(4,128)S(1)} %get-tuple-element.1263), channel_id=1, source_target_pairs={{0,2},{2,4},{4,6},{6,8},{8,10},{10,12},{12,14},{14,0},{1,3},{3,5},... | collective-permute-start | bytes 921608 | tf_op jit(solution)/shard_map/while/body/eval_jaxpr/ppermute | solution.py:20
  1309.7 19.0 collective-permute-start.2
  1309.8 19.0 collective-permute-start.3
  1318.2 13.7 collective-permute-start.10
  1556.6 18.1 collective-permute-start.6
  1559.1 19.5 collective-permute-start.7
  1562.1 30.8 %collective-permute-start = (f32[3,14,10,128]{3,1,2,0:T(8,128)S(1)}, f32[3,14,10,128]{3,1,2,0:T(8,128)S(1)}, u32[]{:S(2)}, u32[]{:S(2)}) collective-permute-start(f32[3,14,10,128]{3,1,2,0:T(8,128)S(1)} %get-tuple-element.1254), channel_id=1, source_target_pairs={{0,16},{16,32},{32,48},{48,64},{64,80},{80,96},{96,112},{112,128},... | collective-permute-start | bytes 645128 | tf_op jit(solution)/shard_map/while/body/eval_jaxpr/ppermute | solution.py:20
  1562.5 38.9 %collective-permute-start.1 = (f32[3,14,10,128]{3,1,2,0:T(8,128)S(1)}, f32[3,14,10,128]{3,1,2,0:T(8,128)S(1)}, u32[]{:S(2)}, u32[]{:S(2)}) collective-permute-start(f32[3,14,10,128]{3,1,2,0:T(8,128)S(1)} %get-tuple-element.1255), channel_id=1, source_target_pairs={{16,0},{32,16},{48,32},{64,48},{80,64},{96,80},{112,96},{128,112},... | collective-permute-start | bytes 645128 | tf_op jit(solution)/shard_map/while/body/eval_jaxpr/ppermute | solution.py:22
  1578.8 24.4 %collective-permute-start.8 = (f32[20,3,10,128]{3,1,2,0:T(4,128)S(1)}, f32[20,3,10,128]{3,1,2,0:T(4,128)S(1)}, u32[]{:S(2)}, u32[]{:S(2)}) collective-permute-start(f32[20,3,10,128]{3,1,2,0:T(4,128)S(1)} %get-tuple-element.1262), channel_id=1, source_target_pairs={{2,0},{4,2},{6,4},{8,6},{10,8},{12,10},{14,12},{0,14},{3,1},{5,3},... | collective-permute-start | bytes 921608 | tf_op jit(solution)/shard_map/while/body/eval_jaxpr/ppermute | solution.py:22
  1578.9 27.3 %collective-permute-start.9 = (f32[20,3,10,128]{3,1,2,0:T(4,128)S(1)}, f32[20,3,10,128]{3,1,2,0:T(4,128)S(1)}, u32[]{:S(2)}, u32[]{:S(2)}) collective-permute-start(f32[20,3,10,128]{3,1,2,0:T(4,128)S(1)} %get-tuple-element.1263), channel_id=1, source_target_pairs={{0,2},{2,4},{4,6},{6,8},{8,10},{10,12},{12,14},{14,0},{1,3},{3,5},... | collective-permute-start | bytes 921608 | tf_op jit(solution)/shard_map/while/body/eval_jaxpr/ppermute | solution.py:20
  1601.7 19.3 collective-permute-start.2
  1601.7 19.2 collective-permute-start.3
  1607.7 16.2 collective-permute-start.10
  1609.7 14.2 collective-permute-start.11
  1848.5 16.1 collective-permute-start.6
  1848.6 19.3 collective-permute-start.7
  1854.0 29.0 %collective-permute-start = (f32[3,14,10,128]{3,1,2,0:T(8,128)S(1)}, f32[3,14,10,128]{3,1,2,0:T(8,128)S(1)}, u32[]{:S(2)}, u32[]{:S(2)}) collective-permute-start(f32[3,14,10,128]{3,1,2,0:T(8,128)S(1)} %get-tuple-element.1254), channel_id=1, source_target_pairs={{0,16},{16,32},{32,48},{48,64},{64,80},{80,96},{96,112},{112,128},... | collective-permute-start | bytes 645128 | tf_op jit(solution)/shard_map/while/body/eval_jaxpr/ppermute | solution.py:20
  1854.1 36.6 %collective-permute-start.1 = (f32[3,14,10,128]{3,1,2,0:T(8,128)S(1)}, f32[3,14,10,128]{3,1,2,0:T(8,128)S(1)}, u32[]{:S(2)}, u32[]{:S(2)}) collective-permute-start(f32[3,14,10,128]{3,1,2,0:T(8,128)S(1)} %get-tuple-element.1255), channel_id=1, source_target_pairs={{16,0},{32,16},{48,32},{64,48},{80,64},{96,80},{112,96},{128,112},... | collective-permute-start | bytes 645128 | tf_op jit(solution)/shard_map/while/body/eval_jaxpr/ppermute | solution.py:22
  1868.1 24.4 %collective-permute-start.8 = (f32[20,3,10,128]{3,1,2,0:T(4,128)S(1)}, f32[20,3,10,128]{3,1,2,0:T(4,128)S(1)}, u32[]{:S(2)}, u32[]{:S(2)}) collective-permute-start(f32[20,3,10,128]{3,1,2,0:T(4,128)S(1)} %get-tuple-element.1262), channel_id=1, source_target_pairs={{2,0},{4,2},{6,4},{8,6},{10,8},{12,10},{14,12},{0,14},{3,1},{5,3},... | collective-permute-start | bytes 921608 | tf_op jit(solution)/shard_map/while/body/eval_jaxpr/ppermute | solution.py:22
  1868.2 28.1 %collective-permute-start.9 = (f32[20,3,10,128]{3,1,2,0:T(4,128)S(1)}, f32[20,3,10,128]{3,1,2,0:T(4,128)S(1)}, u32[]{:S(2)}, u32[]{:S(2)}) collective-permute-start(f32[20,3,10,128]{3,1,2,0:T(4,128)S(1)} %get-tuple-element.1263), channel_id=1, source_target_pairs={{0,2},{2,4},{4,6},{6,8},{8,10},{10,12},{12,14},{14,0},{1,3},{3,5},... | collective-permute-start | bytes 921608 | tf_op jit(solution)/shard_map/while/body/eval_jaxpr/ppermute | solution.py:20
  1890.9 18.0 collective-permute-start.2
  1891.0 17.9 collective-permute-start.3
  1897.7 15.4 collective-permute-start.10
  1898.6 14.5 collective-permute-start.11
  (358 other events, 1887.6 us)
Sparse Core Ops, SparseCore 0:
  1926.4 249.1 all-reduce.17
where the time goes:
time: 2210 us; the launch traced here: 2190 us
  blocking collectives  686 us (31%)
  local copies, waits for them, and re-layouts  561 us (25%)
  waiting for transfers between devices  433 us (20%)
  matrix products  221 us (10%)
  other arithmetic  158 us (7%)
  starting transfers between devices  107 us (5%)
    all_gather x1, blocking collectives, per_device(): lax.all_gather(summary_address_table, ('row', 'aisle', 'height'), axis=0,...  345 us
    all_gather x1, blocking collectives, per_device(): lax.all_gather(summary_content_table, ('row', 'aisle', 'height'), axis=0,...  341 us
    unnamed x2, waiting for transfers between devices  249 us
    while x736, local copies, waits for them, and re-layouts  114 us
    ppermute x33, waiting for transfers between devices, padded(): lax.ppermute(tail, axis, [(i, (i + 1) % count) for i in range(count)])  99.8 us
    ppermute x33, waiting for transfers between devices, padded(): lax.ppermute(head, axis, [((i + 1) % count, i) for i in range(count)])  83.8 us
    reshape x64, local copies, waits for them, and re-layouts, cut_inner(): return piece.reshape(inner, heads_now, level_reach_along)  80.7 us
    ppermute x33, starting transfers between devices, padded(): lax.ppermute(head, axis, [((i + 1) % count, i) for i in range(count)])  69.9 us
  transfers between devices with their start and end apart: 67, of which 33 were waited for; matrix products, arithmetic and copies ran while one was open for 2% of the time, Pallas kernels for 0%

commit v1 on v0

v1 whole, which is shorter than its diff:
```python
import jax
import jax.numpy as jnp
from jax import lax
from jax.experimental import pallas as pl
from jax.experimental.pallas import tpu as pltpu
from jax.sharding import Mesh
from jax.sharding import PartitionSpec as P


HEADS = 8
DIM = 64
REACH = 3
ROWS = 16
WIDE = 16
TALL = 8
BIG_ROWS = ROWS + 2 * REACH
BIG_LINE = (WIDE + 2 * REACH) * TALL
LINE = WIDE * TALL
CARRIERS = 256
SOLID = 64.0
NEGATIVE = -1e30
RING = ("yh", "yl", "core")
ACROSS = ("z", "x")

T_ROWS = 2 + 2 * REACH
T_LINE = (4 + 2 * REACH) * TALL
T_KEYS = T_ROWS * T_LINE
ALL_KEYS = T_KEYS + CARRIERS

NT = (((1,), (1,)), ((), ()))
NN = (((1,), (0,)), ((), ()))
TN = (((0,), (0,)), ((), ()))


def dot(a, b, dims):
    return lax.dot_general(a, b, dims, preferred_element_type=jnp.float32)


def fold8(x, op):
    total = x[0:8]
    for i in range(1, x.shape[0] // 8):
        total = op(total, x[8 * i : 8 * i + 8])
    return total


def attend_kernel(
    place, big, qg, car, dbig, dq, dcar, live, near, scores, grads, low, car_pair, car_sum
):
    f32, bf16 = jnp.float32, jnp.bfloat16
    x_at = place[0]

    spot = lax.broadcasted_iota(jnp.int32, (BIG_LINE, 128), 0) // TALL
    off = ((x_at == 0) & (spot < REACH)) | ((x_at == 3) & (spot >= WIDE + REACH))

    def clear(r, carry):
        mark = big[r, :, 0:128].astype(f32)[:, 0:1]
        live[r] = jnp.where(off | (mark > 0.5 * SOLID), NEGATIVE, 0.0)
        dbig[r] = jnp.zeros((BIG_LINE, 128), f32)
        return carry

    lax.fori_loop(0, BIG_ROWS, clear, 0)
    col = lax.broadcasted_iota(jnp.int32, (T_LINE, 128), 1) & 63
    key = lax.broadcasted_iota(jnp.int32, (T_LINE, 128), 0)
    a_gap = (key >> 3) - ((col >> 3) & 3)
    h_gap = (key & 7) - (col & 7)
    close = (a_gap >= 0) & (a_gap <= 2 * REACH) & (h_gap >= -REACH) & (h_gap <= REACH)
    for r in range(T_ROWS):
        r_gap = r - (col >> 5)
        near[r] = jnp.where(close & (r_gap >= 0) & (r_gap <= 2 * REACH), 0.0, NEGATIVE)
    car_pair[...] = jnp.concatenate([car[...], car[...]], axis=1)
    car_sum[...] = jnp.zeros((CARRIERS, 256), f32)

    w_row = lax.broadcasted_iota(jnp.int32, (256, 256), 0) >> 6
    w_col = lax.broadcasted_iota(jnp.int32, (256, 256), 1) >> 6
    keep = w_col == jnp.where(w_row < 2, 2 * w_row, 2 * w_row - 3)
    first_half = lax.broadcasted_iota(jnp.int32, (T_LINE, 128), 1) < 64

    def turn(i, carry):
        r0 = (i >> 1) * 2
        a0 = pl.multiple_of((i & 1) * 64, 64)
        b0 = pl.multiple_of((i & 1) * 64 + 32, 32)
        asks = jnp.concatenate(
            [
                qg[pl.ds(r0, 2), pl.ds(a0, 32), :].reshape(64, 128),
                qg[pl.ds(r0, 2), pl.ds(b0, 32), :].reshape(64, 128),
            ],
            axis=1,
        )
        weights = jnp.where(keep, jnp.concatenate([asks] * 4, axis=0), 0)

        def keys(r):
            return jnp.concatenate(
                [big[r0 + r, pl.ds(a0, T_LINE), :], big[r0 + r, pl.ds(b0, T_LINE), :]], axis=1
            )

        chunks = [(r * T_LINE, T_LINE) for r in range(T_ROWS)]
        chunks += [(T_KEYS + j * 64, 64) for j in range(CARRIERS // 64)]

        top = jnp.full((8, 128), NEGATIVE, f32)
        for r, (start, size) in enumerate(chunks):
            if r < T_ROWS:
                both = dot(keys(r), weights, NT)
                s = both[:, :128] + (
                    jnp.where(
                        first_half,
                        live[r0 + r, pl.ds(a0, T_LINE), :],
                        live[r0 + r, pl.ds(b0, T_LINE), :],
                    )
                    + near[r]
                )
            else:
                both = dot(car_pair[pl.ds(start - T_KEYS, size), :], weights, NT)
                s = both[:, :128]
            scores[pl.ds(start, size), :] = s
            grads[pl.ds(start, size), :] = both[:, 128:]
            top = jnp.maximum(top, fold8(s, jnp.maximum))
        top = jnp.max(top, axis=0, keepdims=True)

        total = jnp.zeros((8, 128), f32)
        for start, size in chunks:
            e = jnp.exp(scores[pl.ds(start, size), :] - top)
            scores[pl.ds(start, size), :] = e
            total = total + fold8(e, jnp.add)
        share = 1.0 / jnp.sum(total, axis=0, keepdims=True)

        delta = jnp.zeros((8, 128), f32)
        for start, size in chunks:
            p = (scores[pl.ds(start, size), :] * share).astype(bf16)
            low[pl.ds(start, size), 128:] = p
            delta = delta + fold8(p.astype(f32) * grads[pl.ds(start, size), :], jnp.add)
        delta = jnp.sum(delta, axis=0, keepdims=True)

        for start, size in chunks:
            p = scores[pl.ds(start, size), :] * share
            low[pl.ds(start, size), :128] = (p * (grads[pl.ds(start, size), :] - delta)).astype(
                bf16
            )

        back = jnp.zeros((128, 256), f32)
        for r in range(T_ROWS):
            piece = low[pl.ds(r * T_LINE, T_LINE), :]
            part = dot(piece, weights, NN)
            dbig[r0 + r, pl.ds(a0, T_LINE), :] += part[:, :128]
            dbig[r0 + r, pl.ds(b0, T_LINE), :] += part[:, 128:]
        car_sum[...] += dot(low[pl.ds(T_KEYS, CARRIERS), :], weights, NN)
        window = jnp.concatenate([keys(r) for r in range(T_ROWS)], axis=0)
        back = dot(low[pl.ds(0, T_KEYS), :128], window, TN)
        back = back + dot(low[pl.ds(T_KEYS, CARRIERS), :128], car_pair[...], TN)
        back = jnp.concatenate([back[:64, :64], back[64:, 128:192]], axis=1) * DIM**-0.5
        d0 = pl.multiple_of((i & 1) * 32, 32)
        dq[pl.ds(r0, 2), pl.ds(d0, 32), :] = back.reshape(2, 32, 128).astype(bf16)
        return carry

    lax.fori_loop(0, 16, turn, 0)
    dcar[...] = car_sum[:, :128] + car_sum[:, 128:]


def attend(place, big, qg, car):
    f32, bf16 = jnp.float32, jnp.bfloat16
    whole = pl.BlockSpec(memory_space=pltpu.VMEM)
    return pl.pallas_call(
        attend_kernel,
        out_shape=(
            jax.ShapeDtypeStruct((BIG_ROWS, BIG_LINE, 128), f32),
            jax.ShapeDtypeStruct((ROWS, LINE // 2, 128), bf16),
            jax.ShapeDtypeStruct((CARRIERS, 128), f32),
        ),
        in_specs=[pl.BlockSpec(memory_space=pltpu.SMEM), whole, whole, whole],
        out_specs=(whole, whole, whole),
        scratch_shapes=[
            pltpu.VMEM((BIG_ROWS, BIG_LINE, 128), f32),
            pltpu.VMEM((T_ROWS, T_LINE, 128), f32),
            pltpu.VMEM((ALL_KEYS, 128), f32),
            pltpu.VMEM((ALL_KEYS, 128), f32),
            pltpu.VMEM((ALL_KEYS, 256), bf16),
            pltpu.VMEM((CARRIERS, 256), bf16),
            pltpu.VMEM((CARRIERS, 256), f32),
        ],
        compiler_params=pltpu.CompilerParams(vmem_limit_bytes=40 * 2**20),
    )(place, big, qg, car)


def pair_heads(a, b):
    tokens = a.shape[:-1]
    a = a.reshape(-1, HEADS, DIM)
    b = b.reshape(-1, HEADS, DIM)
    return jnp.concatenate([a, b], axis=-1).transpose(1, 0, 2)


def spread(x):
    return lax.all_to_all(x, RING, 0, 0, tiled=True)


def to_block(x):
    x = x.reshape(2, 2, 2, 8, 8, 4, 128)
    return x.transpose(0, 3, 1, 4, 2, 5, 6).reshape(ROWS, WIDE, TALL, 128)


def ring_pairs(n, step):
    return [(i, (i + step) % n) for i in range(n)]


def line_pairs(n, step):
    return [(i, i + step) for i in range(n) if 0 <= i + step < n]


def per_device(q, k, v, g, car_k, car_v, open_cells):
    f32, bf16 = jnp.float32, jnp.bfloat16
    nz, nx = lax.axis_size("z"), lax.axis_size("x")
    k = jnp.where((open_cells > 0)[..., None], k, jnp.bfloat16(SOLID))
    kv = pair_heads(k, v)
    own_car = jnp.pad(pair_heads(car_k, car_v), ((0, 0), (0, 15), (0, 0)))
    kv = spread(jnp.concatenate([kv, own_car], axis=1))
    qg = to_block(spread(pair_heads(q * jnp.bfloat16(DIM**-0.5), g)))
    car = jnp.broadcast_to(kv[None, :, 256], (nz * nx, 8, 128))
    car = lax.all_to_all(car, ACROSS, 0, 0, tiled=True).reshape(CARRIERS, 128)

    own = to_block(kv[:, :256])
    upper = lax.ppermute(own[ROWS - REACH :], "z", ring_pairs(nz, 1))
    lower = lax.ppermute(own[:REACH], "z", ring_pairs(nz, -1))
    big = jnp.concatenate([upper, own, lower], axis=0)
    left = lax.ppermute(big[:, WIDE - REACH :], "x", line_pairs(nx, 1))
    right = lax.ppermute(big[:, :REACH], "x", line_pairs(nx, -1))
    big = jnp.concatenate([left, big, right], axis=1)

    place = lax.axis_index("x").astype(jnp.int32).reshape(1)
    dbig, dq, dcar = attend(
        place, big.reshape(BIG_ROWS, BIG_LINE, 128), qg.reshape(ROWS, LINE, 128), car
    )

    dcar = lax.all_to_all(dcar.reshape(nz * nx, 8, 128), ACROSS, 0, 0, tiled=True)
    dq = dq.reshape(2, 8, 2, 4, 2, 4, 128).transpose(0, 2, 4, 1, 3, 5, 6)
    dq = spread(dq.reshape(8, 128, 128))
    dq = dq.reshape(HEADS, 8, 4, 4, 2, DIM).transpose(1, 4, 2, 3, 0, 5).reshape(8, 8, 4, 512)

    dbig = dbig.reshape(BIG_ROWS, WIDE + 2 * REACH, TALL, 128)
    from_left = lax.ppermute(
        dbig[:, WIDE + REACH :].astype(bf16), "x", line_pairs(nx, 1)
    ).astype(f32)
    from_right = lax.ppermute(dbig[:, :REACH].astype(bf16), "x", line_pairs(nx, -1)).astype(f32)
    rest = WIDE - REACH
    mid = (
        dbig[:, REACH : WIDE + REACH]
        + jnp.pad(from_left, ((0, 0), (0, rest), (0, 0), (0, 0)))
        + jnp.pad(from_right, ((0, 0), (rest, 0), (0, 0), (0, 0)))
    )
    from_up = lax.ppermute(
        mid[ROWS + REACH :].astype(bf16), "z", ring_pairs(nz, 1)
    ).astype(f32)
    from_down = lax.ppermute(mid[:REACH].astype(bf16), "z", ring_pairs(nz, -1)).astype(f32)
    rest = ROWS - REACH
    dkv = (
        mid[REACH : ROWS + REACH]
        + jnp.pad(from_up, ((0, rest), (0, 0), (0, 0), (0, 0)))
        + jnp.pad(from_down, ((rest, 0), (0, 0), (0, 0), (0, 0)))
    ).astype(bf16)
    dkv = dkv.reshape(2, 8, 2, 8, 2, 4, 128).transpose(0, 2, 4, 1, 3, 5, 6).reshape(8, 256, 128)
    dcar = jnp.sum(dcar, axis=0)
    car_high = dcar.astype(bf16)
    car_low = (dcar - car_high.astype(f32)).astype(bf16)
    extra = jnp.pad(jnp.stack([car_high, car_low], axis=1), ((0, 0), (0, 14), (0, 0)))
    dkv = spread(jnp.concatenate([dkv, extra], axis=1))
    dcar = dkv[:, 256].astype(f32) + dkv[:, 257].astype(f32)
    dkv = dkv[:, :256].transpose(1, 0, 2)
    dk = dkv[..., :DIM].reshape(8, 8, 4, 512)
    dv = dkv[..., DIM:].reshape(8, 8, 4, 512)
    return dq, dk, dv, dcar[:, :DIM].reshape(1, 512), dcar[:, DIM:].reshape(1, 512)


def solution(mesh):
    fine = Mesh(mesh.devices.reshape(-1, 2, 4, 2, 2), ("z", "yh", "x", "yl", "core"))
    tokens = P(("z", "yh"), ("x", "yl"), "core", None)
    carriers = P(("z", "yh", "x", "yl", "core"), None)
    return jax.shard_map(
        per_device,
        mesh=fine,
        in_specs=(tokens, tokens, tokens, tokens, carriers, carriers, P(*tokens[:3])),
        out_specs=(tokens, tokens, tokens, carriers, carriers),
        check_vma=False,
    )
```

time: 2210 us -> 145 us (0.07); the launches traced: 2190 us -> 144 us
  blocking collectives: 686 us -> 0 us
  local copies, waits for them, and re-layouts: 561 us -> 11.4 us
  waiting for transfers between devices: 433 us -> 46.8 us
  matrix products: 221 us -> 0 us
  other arithmetic: 158 us -> 5.77 us
  starting transfers between devices: 107 us -> 55 us
  Pallas kernels: 0 us -> 24.4 us
    all_gather x2 -> x0, blocking collectives: 686 us -> none  [the longest x1 345 us: per_device(): lax.all_gather(summary_address_table, ('row', 'aisle', 'height'), axis=0,...]
    unnamed x2 -> x0, waiting for transfers between devices: 249 us -> none
    dot_general x192 -> x0, matrix products: 221 us -> none  [the longest x16 32 us: query_pass(): jnp.einsum('nqk,knd->qnd', attend_low, value_section, preferred_element_t...]
    reshape x144 -> x13, local copies, waits for them, and re-layouts: 223 us -> 5.84 us  [the longest x1 1 us: per_device(): dv = dkv[..., DIM:].reshape(8, 8, 4, 512)]
    ppermute x66 -> x8, waiting for transfers between devices: 184 us -> 7.41 us  [the longest x1 3.79 us: per_device(): lax.ppermute(dbig[:, :REACH].astype(bf16), 'x', line_pairs(nx, -1))]
    while x751 -> x0, local copies, waits for them, and re-layouts: 129 us -> none
    ppermute x66 -> x8, starting transfers between devices: 107 us -> 15.7 us  [the longest x1 4.03 us: per_device(): lower = lax.ppermute(own[:REACH], 'z', ring_pairs(nz, -1))]
    slice x73 -> x9, local copies, waits for them, and re-layouts: 78 us -> 1.08 us  [the longest x2 0.57 us: per_device(): dv = dkv[..., DIM:].reshape(8, 8, 4, 512)]
  transfers between devices with their start and end apart: 67 -> 14, of which waited for: 33 -> 8; matrix products, arithmetic and copies ran while one was open for 2% -> 5% of each run, Pallas kernels for 0% -> 0%
where the time goes in v1:
time: 145 us; the launch traced here: 144 us
  starting transfers between devices  55 us (38%)
  waiting for transfers between devices  46.8 us (32%)
  Pallas kernels  24.4 us (17%)
  local copies, waits for them, and re-layouts  11.4 us (8%)
  other arithmetic  5.77 us (4%)
    all_to_all x4, starting transfers between devices, spread(): return lax.all_to_all(x, RING, 0, 0, tiled=True)  26 us
    pallas_call x1, Pallas kernels, attend(): pl.pallas_call(attend_kernel, out_shape=(jax.ShapeDtypeStruct((BIG_ROWS,...  24.4 us
    all_to_all x4, waiting for transfers between devices, spread(): return lax.all_to_all(x, RING, 0, 0, tiled=True)  21.8 us
    all_to_all x1, waiting for transfers between devices, per_device(): lax.all_to_all(dcar.reshape(nz * nx, 8, 128), ACROSS, 0, 0, tiled=True)  9 us
    all_to_all x1, starting transfers between devices, per_device(): car = lax.all_to_all(car, ACROSS, 0, 0, tiled=True).reshape(CARRIERS, 128)  8.85 us
    all_to_all x1, waiting for transfers between devices, per_device(): car = lax.all_to_all(car, ACROSS, 0, 0, tiled=True).reshape(CARRIERS, 128)  8.61 us
    all_to_all x1, starting transfers between devices, per_device(): lax.all_to_all(dcar.reshape(nz * nx, 8, 128), ACROSS, 0, 0, tiled=True)  4.48 us
    ppermute x1, starting transfers between devices, per_device(): lower = lax.ppermute(own[:REACH], 'z', ring_pairs(nz, -1))  4.03 us
  transfers between devices with their start and end apart: 14, of which 8 were waited for; matrix products, arithmetic and copies ran while one was open for 5% of the time, Pallas kernels for 0%

profile of v1, /device:TPU:1, one launch (start us, length us, event | category | flops | bytes accessed | tf_op | source)
XLA Modules:
  0.0 144.3 jit_solution(16505679050217224011)
XLA Ops:
  0.6 0.7 reduce
  1.5 0.7 reduce.1
  2.3 0.7 broadcast_compare_fusion
  3.1 1.1 broadcast_select_fusion
  4.3 0.3 reshape.108
  4.6 0.3 reshape.109
  4.9 0.3 maximum_bitcast_fusion.1
  5.3 0.9 copy.41
  6.2 6.8 %all-to-all-start = ((bf16[8,272,128]{2,1,0:T(8,128)(2,1)}), bf16[8,272,128]{2,1,0:T(8,128)(2,1)S(1)}, u32[]{:S(2)}, u32[]{:S(2)}) async-start(bf16[8,272,128]{2,1,0:T(8,128)(2,1)} %copy.41), calls=%async_computation | async-start | bytes 1114112 | tf_op jit(solution)/shard_map/all_to_all | solution.py:191
  13.1 0.3 reshape.115
  13.4 0.3 reshape.116
  13.7 0.3 maximum_bitcast_fusion.2
  14.0 0.9 copy.43
  14.9 8.0 %all-to-all-done = bf16[8,272,128]{2,1,0:T(8,128)(2,1)S(1)} async-done(((bf16[8,272,128]{2,1,0:T(8,128)(2,1)}), bf16[8,272,128]{2,1,0:T(8,128)(2,1)S(1)}, u32[]{:S(2)}, u32[]{:S(2)}) %all-to-all-start) | async-done | bytes 557088 | tf_op jit(solution)/shard_map/all_to_all | solution.py:191
  22.8 4.3 %all-to-all-start.1 = ((bf16[8,256,128]{2,1,0:T(8,128)(2,1)}), bf16[8,256,128]{2,1,0:T(8,128)(2,1)S(1)}, u32[]{:S(2)}, u32[]{:S(2)}) async-start(bf16[8,256,128]{2,1,0:T(8,128)(2,1)} %copy.43), calls=%async_computation.1 | async-start | bytes 1048576 | tf_op jit(solution)/shard_map/all_to_all | solution.py:191
  27.1 0.3 copy.42
  27.4 1.0 collective-permute-start
  28.5 4.0 %collective-permute-start.1 = (bf16[3,16,8,128]{3,2,1,0:T(8,128)(2,1)S(1)}, bf16[3,16,8,128]{3,2,1,0:T(8,128)(2,1)S(1)}, u32[]{:S(2)}, u32[]{:S(2)}) collective-permute-start(bf16[3,16,8,128]{3,2,1,0:T(8,128)(2,1)S(1)} %get-tuple-element.37), channel_id=1, source_target_pairs={{0,224},{32,0},{64,32},{96,64},{128,96},{160,128},{192,160},{224,1... | collective-permute-start | bytes 294920 | tf_op jit(solution)/shard_map/ppermute | solution.py:220
  32.5 2.9 %collective-permute-done = bf16[3,16,8,128]{3,2,1,0:T(8,128)(2,1)S(1)} collective-permute-done((bf16[3,16,8,128]{3,2,1,0:T(8,128)(2,1)S(1)}, bf16[3,16,8,128]{3,2,1,0:T(8,128)(2,1)S(1)}, u32[]{:S(2)}, u32[]{:S(2)}) %collective-permute-start) | collective-permute-done | bytes 98336 | tf_op jit(solution)/shard_map/ppermute | solution.py:219
  35.5 3.1 %collective-permute-start.2 = (bf16[22,3,8,128]{3,2,1,0:T(8,128)(2,1)S(1)}, bf16[22,3,8,128]{3,2,1,0:T(8,128)(2,1)S(1)}, u32[]{:S(2)}, u32[]{:S(2)}) collective-permute-start(bf16[22,3,8,128]{3,2,1,0:T(8,128)(2,1)S(1)} %get-tuple-element.32), channel_id=1, source_target_pairs={{0,4},{4,8},{8,12},{1,5},{5,9},{9,13},{2,6},{6,10},{10,14},{3,7},{... | collective-permute-start | bytes 405512 | tf_op jit(solution)/shard_map/ppermute | solution.py:222
  38.6 1.3 collective-permute-start.3
  39.9 0.3 copy.44
  40.2 0.6 broadcast_in_dim.23
  40.9 8.8 %all-to-all-start.2 = ((bf16[32,8,128]{2,1,0:T(8,128)(2,1)}), bf16[32,8,128]{2,1,0:T(8,128)(2,1)S(1)}, u32[]{:S(2)}, u32[]{:S(2)}) async-start(bf16[32,8,128]{2,1,0:T(8,128)(2,1)} %broadcast_in_dim.23), calls=%async_computation.2 | async-start | bytes 131072 | tf_op jit(solution)/shard_map/all_to_all | solution.py:216
  49.9 8.6 %all-to-all-done.2 = bf16[32,8,128]{2,1,0:T(8,128)(2,1)S(1)} async-done(((bf16[32,8,128]{2,1,0:T(8,128)(2,1)}), bf16[32,8,128]{2,1,0:T(8,128)(2,1)S(1)}, u32[]{:S(2)}, u32[]{:S(2)}) %all-to-all-start.2) | async-done | bytes 65568 | tf_op jit(solution)/shard_map/all_to_all | solution.py:216
  58.5 24.4 %shard_map.110 = (f32[22,176,128]{2,1,0:T(8,128)S(1)}, bf16[16,64,128]{2,1,0:T(8,128)(2,1)S(1)}, f32[256,128]{1,0:T(8,128)}) custom-call(s32[1]{0:T(128)} %bitcast.place, bf16[22,176,128]{2,1,0:T(8,128)(2,1)S(1)} %maximum_bitcast_fusion.big, bf16[16,128,128]{2,1,0:T(8,128)(2,1)S(1)} %bitcast.40, bf16[256,128]{1,0:T(8,128)(2,1)S(1)} %bitcast.41), custom_call_target="tpu_custom_call" | custom-call | tf_op jit(solution)/shard_map/pallas_call | solution.py:161
  83.1 2.2 %collective-permute-start.4 = (bf16[22,3,8,128]{3,2,1,0:T(8,128)(2,1)S(1)}, bf16[22,3,8,128]{3,2,1,0:T(8,128)(2,1)S(1)}, u32[]{:S(2)}, u32[]{:S(2)}) collective-permute-start(bf16[22,3,8,128]{3,2,1,0:T(8,128)(2,1)S(1)} %get-tuple-element.28), channel_id=1, source_target_pairs={{0,4},{4,8},{8,12},{1,5},{5,9},{9,13},{2,6},{6,10},{10,14},{3,7},{... | collective-permute-start | bytes 405512 | tf_op jit(solution)/shard_map/ppermute | solution.py:237
  85.2 1.3 collective-permute-start.5
  86.5 0.7 collective-permute-done.4
  87.2 3.8 %collective-permute-done.5 = bf16[22,3,8,128]{3,2,1,0:T(8,128)(2,1)S(1)} collective-permute-done((bf16[22,3,8,128]{3,2,1,0:T(8,128)(2,1)S(1)}, bf16[22,3,8,128]{3,2,1,0:T(8,128)(2,1)S(1)}, u32[]{:S(2)}, u32[]{:S(2)}) %collective-permute-start.5) | collective-permute-done | bytes 135200 | tf_op jit(solution)/shard_map/ppermute | solution.py:240
  91.3 0.7 collective-permute-start.6
  92.0 2.1 %collective-permute-start.7 = (bf16[3,16,8,128]{3,2,1,0:T(8,128)(2,1)S(1)}, bf16[3,16,8,128]{3,2,1,0:T(8,128)(2,1)S(1)}, u32[]{:S(2)}, u32[]{:S(2)}) collective-permute-start(bf16[3,16,8,128]{3,2,1,0:T(8,128)(2,1)S(1)} %get-tuple-element.31), channel_id=1, source_target_pairs={{0,224},{32,0},{64,32},{96,64},{128,96},{160,128},{192,160},{224,1... | collective-permute-start | bytes 294920 | tf_op jit(solution)/shard_map/ppermute | solution.py:250
  94.0 0.8 copy.46
  94.8 4.5 %all-to-all-start.4 = ((f32[32,8,128]{2,1,0:T(8,128)}), f32[32,8,128]{2,1,0:T(8,128)S(1)}, u32[]{:S(2)}, u32[]{:S(2)}) async-start(f32[32,8,128]{2,1,0:T(8,128)} %bitcast.21), calls=%async_computation.4 | async-start | bytes 262144 | tf_op jit(solution)/shard_map/all_to_all | solution.py:231
  99.7 9.0 %all-to-all-done.4 = f32[32,8,128]{2,1,0:T(8,128)S(1)} async-done(((f32[32,8,128]{2,1,0:T(8,128)}), f32[32,8,128]{2,1,0:T(8,128)S(1)}, u32[]{:S(2)}, u32[]{:S(2)}) %all-to-all-start.4) | async-done | bytes 131104 | tf_op jit(solution)/shard_map/all_to_all | solution.py:231
  108.7 10.5 %all-to-all-start.3 = ((bf16[8,128,128]{2,1,0:T(8,128)(2,1)}), bf16[8,128,128]{2,1,0:T(8,128)(2,1)S(1)}, u32[]{:S(2)}, u32[]{:S(2)}) async-start(bf16[8,128,128]{2,1,0:T(8,128)(2,1)} %bitcast.15), calls=%async_computation.3 | async-start | bytes 524288 | tf_op jit(solution)/shard_map/all_to_all | solution.py:191
  119.2 0.9 pad_maximum_fusion
  120.1 5.6 %all-to-all-done.3 = bf16[8,128,128]{2,1,0:T(8,128)(2,1)S(1)} async-done(((bf16[8,128,128]{2,1,0:T(8,128)(2,1)}), bf16[8,128,128]{2,1,0:T(8,128)(2,1)S(1)}, u32[]{:S(2)}, u32[]{:S(2)}) %all-to-all-start.3) | async-done | bytes 262176 | tf_op jit(solution)/shard_map/all_to_all | solution.py:191
  125.6 4.5 %all-to-all-start.5 = ((bf16[8,272,128]{2,1,0:T(8,128)(2,1)}), bf16[8,272,128]{2,1,0:T(8,128)(2,1)S(1)}, u32[]{:S(2)}, u32[]{:S(2)}) async-start(bf16[8,272,128]{2,1,0:T(8,128)(2,1)} %pad_maximum_fusion), calls=%async_computation.5 | async-start | bytes 1114112 | tf_op jit(solution)/shard_map/all_to_all | solution.py:191
  130.4 0.3 copy.52
  130.7 1.0 reshape.131
  131.7 8.2 %all-to-all-done.5 = bf16[8,272,128]{2,1,0:T(8,128)(2,1)S(1)} async-done(((bf16[8,272,128]{2,1,0:T(8,128)(2,1)}), bf16[8,272,128]{2,1,0:T(8,128)(2,1)S(1)}, u32[]{:S(2)}, u32[]{:S(2)}) %all-to-all-start.5) | async-done | bytes 557088 | tf_op jit(solution)/shard_map/all_to_all | solution.py:191
  140.0 0.7 reshape.130
  140.7 0.7 reshape.129
  141.6 0.3 copy.50
  142.0 1.0 reshape.128
  143.0 0.3 copy.49
  143.3 1.0 reshape.127
  (39 shorter events, 2.2 us)
Async XLA Ops:
  0.6 3.9 %copy-start = (bf16[8,8,4,512]{3,2,1,0:T(4,128)(2,1)S(1)}, bf16[8,8,4,512]{3,2,1,0:T(4,128)(2,1)}, u32[]{:S(2)}) copy-start(bf16[8,8,4,512]{3,2,1,0:T(4,128)(2,1)} %param.9) | copy-start | bytes 786436
  5.2 7.8 %copy-start.2 = (bf16[8,8,4,512]{3,2,1,0:T(4,128)(2,1)S(1)}, bf16[8,8,4,512]{3,2,1,0:T(4,128)(2,1)}, u32[]{:S(2)}) copy-start(bf16[8,8,4,512]{3,2,1,0:T(4,128)(2,1)} %param.7) | copy-start | bytes 786436
  6.2 7.2 %copy-start.1 = (bf16[8,8,4,512]{3,2,1,0:T(4,128)(2,1)S(1)}, bf16[8,8,4,512]{3,2,1,0:T(4,128)(2,1)}, u32[]{:S(2)}) copy-start(bf16[8,8,4,512]{3,2,1,0:T(4,128)(2,1)} %param.10) | copy-start | bytes 786436
  6.2 16.7 %all-to-all-start = ((bf16[8,272,128]{2,1,0:T(8,128)(2,1)}), bf16[8,272,128]{2,1,0:T(8,128)(2,1)S(1)}, u32[]{:S(2)}, u32[]{:S(2)}) async-start(bf16[8,272,128]{2,1,0:T(8,128)(2,1)} %copy.41), calls=%async_computation | async-start | bytes 1114112 | tf_op jit(solution)/shard_map/all_to_all | solution.py:191
  22.8 17.1 %all-to-all-start.1 = ((bf16[8,256,128]{2,1,0:T(8,128)(2,1)}), bf16[8,256,128]{2,1,0:T(8,128)(2,1)S(1)}, u32[]{:S(2)}, u32[]{:S(2)}) async-start(bf16[8,256,128]{2,1,0:T(8,128)(2,1)} %copy.43), calls=%async_computation.1 | async-start | bytes 1048576 | tf_op jit(solution)/shard_map/all_to_all | solution.py:191
  27.4 8.0 %collective-permute-start = (bf16[3,16,8,128]{3,2,1,0:T(8,128)(2,1)S(1)}, bf16[3,16,8,128]{3,2,1,0:T(8,128)(2,1)S(1)}, u32[]{:S(2)}, u32[]{:S(2)}) collective-permute-start(bf16[3,16,8,128]{3,2,1,0:T(8,128)(2,1)S(1)} %get-tuple-element.36), channel_id=1, source_target_pairs={{0,32},{32,64},{64,96},{96,128},{128,160},{160,192},{192,224},{224... | collective-permute-start | bytes 294920 | tf_op jit(solution)/shard_map/ppermute | solution.py:219
  28.5 7.0 %collective-permute-start.1 = (bf16[3,16,8,128]{3,2,1,0:T(8,128)(2,1)S(1)}, bf16[3,16,8,128]{3,2,1,0:T(8,128)(2,1)S(1)}, u32[]{:S(2)}, u32[]{:S(2)}) collective-permute-start(bf16[3,16,8,128]{3,2,1,0:T(8,128)(2,1)S(1)} %get-tuple-element.37), channel_id=1, source_target_pairs={{0,224},{32,0},{64,32},{96,64},{128,96},{160,128},{192,160},{224,1... | collective-permute-start | bytes 294920 | tf_op jit(solution)/shard_map/ppermute | solution.py:220
  35.5 14.2 %collective-permute-start.2 = (bf16[22,3,8,128]{3,2,1,0:T(8,128)(2,1)S(1)}, bf16[22,3,8,128]{3,2,1,0:T(8,128)(2,1)S(1)}, u32[]{:S(2)}, u32[]{:S(2)}) collective-permute-start(bf16[22,3,8,128]{3,2,1,0:T(8,128)(2,1)S(1)} %get-tuple-element.32), channel_id=1, source_target_pairs={{0,4},{4,8},{8,12},{1,5},{5,9},{9,13},{2,6},{6,10},{10,14},{3,7},{... | collective-permute-start | bytes 405512 | tf_op jit(solution)/shard_map/ppermute | solution.py:222
  38.6 11.1 %collective-permute-start.3 = (bf16[22,3,8,128]{3,2,1,0:T(8,128)(2,1)S(1)}, bf16[22,3,8,128]{3,2,1,0:T(8,128)(2,1)S(1)}, u32[]{:S(2)}, u32[]{:S(2)}) collective-permute-start(bf16[22,3,8,128]{3,2,1,0:T(8,128)(2,1)S(1)} %get-tuple-element.33), channel_id=1, source_target_pairs={{4,0},{8,4},{12,8},{5,1},{9,5},{13,9},{6,2},{10,6},{14,10},{7,3},{... | collective-permute-start | bytes 405512 | tf_op jit(solution)/shard_map/ppermute | solution.py:223
  40.9 17.7 %all-to-all-start.2 = ((bf16[32,8,128]{2,1,0:T(8,128)(2,1)}), bf16[32,8,128]{2,1,0:T(8,128)(2,1)S(1)}, u32[]{:S(2)}, u32[]{:S(2)}) async-start(bf16[32,8,128]{2,1,0:T(8,128)(2,1)} %broadcast_in_dim.23), calls=%async_computation.2 | async-start | bytes 131072 | tf_op jit(solution)/shard_map/all_to_all | solution.py:216
  83.1 4.1 %collective-permute-start.4 = (bf16[22,3,8,128]{3,2,1,0:T(8,128)(2,1)S(1)}, bf16[22,3,8,128]{3,2,1,0:T(8,128)(2,1)S(1)}, u32[]{:S(2)}, u32[]{:S(2)}) collective-permute-start(bf16[22,3,8,128]{3,2,1,0:T(8,128)(2,1)S(1)} %get-tuple-element.28), channel_id=1, source_target_pairs={{0,4},{4,8},{8,12},{1,5},{5,9},{9,13},{2,6},{6,10},{10,14},{3,7},{... | collective-permute-start | bytes 405512 | tf_op jit(solution)/shard_map/ppermute | solution.py:237
  85.2 5.8 %collective-permute-start.5 = (bf16[22,3,8,128]{3,2,1,0:T(8,128)(2,1)S(1)}, bf16[22,3,8,128]{3,2,1,0:T(8,128)(2,1)S(1)}, u32[]{:S(2)}, u32[]{:S(2)}) collective-permute-start(bf16[22,3,8,128]{3,2,1,0:T(8,128)(2,1)S(1)} %get-tuple-element.29), channel_id=1, source_target_pairs={{4,0},{8,4},{12,8},{5,1},{9,5},{13,9},{6,2},{10,6},{14,10},{7,3},{... | collective-permute-start | bytes 405512 | tf_op jit(solution)/shard_map/ppermute | solution.py:240
  91.3 8.1 %collective-permute-start.6 = (bf16[3,16,8,128]{3,2,1,0:T(8,128)(2,1)S(1)}, bf16[3,16,8,128]{3,2,1,0:T(8,128)(2,1)S(1)}, u32[]{:S(2)}, u32[]{:S(2)}) collective-permute-start(bf16[3,16,8,128]{3,2,1,0:T(8,128)(2,1)S(1)} %get-tuple-element.30), channel_id=1, source_target_pairs={{0,32},{32,64},{64,96},{96,128},{128,160},{160,192},{192,224},{224... | collective-permute-start | bytes 294920 | tf_op jit(solution)/shard_map/ppermute | solution.py:247
  92.0 7.4 %collective-permute-start.7 = (bf16[3,16,8,128]{3,2,1,0:T(8,128)(2,1)S(1)}, bf16[3,16,8,128]{3,2,1,0:T(8,128)(2,1)S(1)}, u32[]{:S(2)}, u32[]{:S(2)}) collective-permute-start(bf16[3,16,8,128]{3,2,1,0:T(8,128)(2,1)S(1)} %get-tuple-element.31), channel_id=1, source_target_pairs={{0,224},{32,0},{64,32},{96,64},{128,96},{160,128},{192,160},{224,1... | collective-permute-start | bytes 294920 | tf_op jit(solution)/shard_map/ppermute | solution.py:250
  94.8 13.8 %all-to-all-start.4 = ((f32[32,8,128]{2,1,0:T(8,128)}), f32[32,8,128]{2,1,0:T(8,128)S(1)}, u32[]{:S(2)}, u32[]{:S(2)}) async-start(f32[32,8,128]{2,1,0:T(8,128)} %bitcast.21), calls=%async_computation.4 | async-start | bytes 262144 | tf_op jit(solution)/shard_map/all_to_all | solution.py:231
  108.7 17.0 %all-to-all-start.3 = ((bf16[8,128,128]{2,1,0:T(8,128)(2,1)}), bf16[8,128,128]{2,1,0:T(8,128)(2,1)S(1)}, u32[]{:S(2)}, u32[]{:S(2)}) async-start(bf16[8,128,128]{2,1,0:T(8,128)(2,1)} %bitcast.15), calls=%async_computation.3 | async-start | bytes 524288 | tf_op jit(solution)/shard_map/all_to_all | solution.py:191
  125.6 14.3 %all-to-all-start.5 = ((bf16[8,272,128]{2,1,0:T(8,128)(2,1)}), bf16[8,272,128]{2,1,0:T(8,128)(2,1)S(1)}, u32[]{:S(2)}, u32[]{:S(2)}) async-start(bf16[8,272,128]{2,1,0:T(8,128)(2,1)} %pad_maximum_fusion), calls=%async_computation.5 | async-start | bytes 1114112 | tf_op jit(solution)/shard_map/all_to_all | solution.py:191

commit v2 on v1

v2 whole, which is shorter than its diff:
```python
import jax
import jax.numpy as jnp
from jax import lax
from jax.experimental import pallas as pl
from jax.experimental.pallas import tpu as pltpu
from jax.sharding import Mesh
from jax.sharding import PartitionSpec as P


HEADS = 8
DIM = 64
REACH = 3
ROWS = 16
WIDE = 16
TALL = 8
BIG_ROWS = ROWS + 2 * REACH
BIG_LINE = (WIDE + 2 * REACH) * TALL
LINE = WIDE * TALL
CARRIERS = 256
SOLID = 64.0
NEGATIVE = -1e30

RING = ("yh", "yl", "core")

T_ROWS = 2 + 2 * REACH
T_LINE = (4 + 2 * REACH) * TALL
T_KEYS = T_ROWS * T_LINE
ALL_KEYS = T_KEYS + CARRIERS

NT = (((1,), (1,)), ((), ()))
NN = (((1,), (0,)), ((), ()))
TN = (((0,), (0,)), ((), ()))


def dot(a, b, dims):
    return lax.dot_general(a, b, dims, preferred_element_type=jnp.float32)


def fold8(x, op):
    total = x[0:8]
    for i in range(1, x.shape[0] // 8):
        total = op(total, x[8 * i : 8 * i + 8])
    return total


def attend_kernel(
    place, big, qg, car, dbig, dq, dcar, live, near, scores, grads, low, car_pair, car_sum
):
    f32, bf16 = jnp.float32, jnp.bfloat16
    x_at = place[0]

    spot = lax.broadcasted_iota(jnp.int32, (BIG_LINE, 128), 0) // TALL
    off = ((x_at == 0) & (spot < REACH)) | ((x_at == 3) & (spot >= WIDE + REACH))

    outside = jnp.where(off, NEGATIVE, 0.0)
    for r in range(BIG_ROWS):
        mark = big[r].astype(f32)[:, 0:1]
        live[r] = jnp.where(mark > 0.5 * SOLID, NEGATIVE, outside)
        dbig[r] = jnp.zeros((BIG_LINE, 128), f32)
    col = lax.broadcasted_iota(jnp.int32, (T_LINE, 128), 1) & 63
    key = lax.broadcasted_iota(jnp.int32, (T_LINE, 128), 0)
    a_gap = (key >> 3) - ((col >> 3) & 3)
    h_gap = (key & 7) - (col & 7)
    close = (a_gap >= 0) & (a_gap <= 2 * REACH) & (h_gap >= -REACH) & (h_gap <= REACH)
    for r in range(T_ROWS):
        r_gap = r - (col >> 5)
        near[r] = jnp.where(close & (r_gap >= 0) & (r_gap <= 2 * REACH), 0.0, NEGATIVE)
    car_pair[...] = jnp.concatenate([car[...], car[...]], axis=1)
    car_sum[...] = jnp.zeros((CARRIERS, 256), f32)

    w_row = lax.broadcasted_iota(jnp.int32, (256, 256), 0) >> 6
    w_col = lax.broadcasted_iota(jnp.int32, (256, 256), 1) >> 6
    keep = w_col == jnp.where(w_row < 2, 2 * w_row, 2 * w_row - 3)
    first_half = lax.broadcasted_iota(jnp.int32, (T_LINE, 128), 1) < 64

    def turn(i, carry):
        tiles = [setup(4 * i + n, n) for n in range(4)]
        for t in tiles: forward(t)
        for t in tiles: expo(t)
        for t in tiles: lowp(t)
        for t in tiles: dscore(t)
        for t in tiles: backward(t)
        return carry

    chunks = [(r * T_LINE, 8*T_LINE) for r in range(0, T_ROWS, 8)]
    chunks += [(T_KEYS + j, 256) for j in range(0, CARRIERS, 256)]

    def setup(j, n):
        t = dict(n=n)
        t["r0"] = r0 = (j >> 1) * 2
        t["a0"] = a0 = pl.multiple_of((j & 1) * 64, 64)
        t["b0"] = b0 = pl.multiple_of((j & 1) * 64 + 32, 32)
        t["d0"] = pl.multiple_of((j & 1) * 32, 32)
        asks = jnp.concatenate(
            [
                qg[pl.ds(r0, 2), pl.ds(a0, 32), :].reshape(64, 128),
                qg[pl.ds(r0, 2), pl.ds(b0, 32), :].reshape(64, 128),
            ],
            axis=1,
        )
        t["w"] = jnp.where(keep, jnp.concatenate([asks] * 4, axis=0), 0)
        return t

    def keys(t, r, n):
        a = big[pl.ds(t["r0"] + r, n), pl.ds(t["a0"], T_LINE), :].reshape(n * T_LINE, 128)
        b = big[pl.ds(t["r0"] + r, n), pl.ds(t["b0"], T_LINE), :].reshape(n * T_LINE, 128)
        return jnp.concatenate([a, b], axis=1)

    def forward(t):
        n = t["n"]
        top = jnp.full((8, 128), NEGATIVE, f32)
        for start, size in chunks:
            if start < T_KEYS:
                r = start // T_LINE
                m = size // T_LINE
                both = dot(keys(t, r, m), t["w"], NT)
                parts = []
                for k in range(m):
                    parts.append(both[k*T_LINE:(k+1)*T_LINE, :128] + (
                        jnp.where(
                            first_half,
                            live[t["r0"] + r + k, pl.ds(t["a0"], T_LINE), :],
                            live[t["r0"] + r + k, pl.ds(t["b0"], T_LINE), :],
                        )
                        + near[r + k]
                    ))
                s = jnp.concatenate(parts, axis=0)
            else:
                both = dot(car_pair[pl.ds(start - T_KEYS, size), :], t["w"], NT)
                s = both[:, :128]
            scores[n, pl.ds(start, size), :] = s
            grads[n, pl.ds(start, size), :] = both[:, 128:]
            top = jnp.maximum(top, fold8(s, jnp.maximum))
        t["top"] = jnp.max(top, axis=0, keepdims=True)

    def expo(t):
        n = t["n"]
        total = jnp.zeros((8, 128), f32)
        for start, size in chunks:
            e = jnp.exp(scores[n, pl.ds(start, size), :] - t["top"])
            scores[n, pl.ds(start, size), :] = e
            total = total + fold8(e, jnp.add)
        t["share"] = 1.0 / jnp.sum(total, axis=0, keepdims=True)

    def lowp(t):
        n = t["n"]
        delta = jnp.zeros((8, 128), f32)
        for start, size in chunks:
            p = (scores[n, pl.ds(start, size), :] * t["share"]).astype(bf16)
            low[n, pl.ds(start, size), 128:] = p
            delta = delta + fold8(p.astype(f32) * grads[n, pl.ds(start, size), :], jnp.add)
        t["delta"] = jnp.sum(delta, axis=0, keepdims=True)

    def dscore(t):
        n = t["n"]
        for start, size in chunks:
            p = scores[n, pl.ds(start, size), :] * t["share"]
            low[n, pl.ds(start, size), :128] = (p * (grads[n, pl.ds(start, size), :] - t["delta"])).astype(bf16)

    def backward(t):
        n = t["n"]
        r0, a0, b0 = t["r0"], t["a0"], t["b0"]
        part = dot(low[n, pl.ds(0, T_KEYS), :], t["w"], NN)
        for r in range(T_ROWS):
            dbig[r0 + r, pl.ds(a0, T_LINE), :] += part[r*T_LINE:(r+1)*T_LINE, :128]
            dbig[r0 + r, pl.ds(b0, T_LINE), :] += part[r*T_LINE:(r+1)*T_LINE, 128:]
        car_sum[...] += dot(low[n, pl.ds(T_KEYS, CARRIERS), :], t["w"], NN)
        back = dot(low[n, pl.ds(0, T_KEYS), :128], keys(t, 0, T_ROWS), TN)
        back = back + dot(low[n, pl.ds(T_KEYS, CARRIERS), :128], car_pair[...], TN)
        back = jnp.concatenate([back[:64, :64], back[64:, 128:192]], axis=1) * DIM**-0.5
        dq[pl.ds(r0, 2), pl.ds(t["d0"], 32), :] = back.reshape(2, 32, 128).astype(bf16)

    lax.fori_loop(0, 16 // 4, turn, 0)
    dcar[...] = car_sum[:, :128] + car_sum[:, 128:]


def attend(place, big, qg, car):
    f32, bf16 = jnp.float32, jnp.bfloat16
    whole = pl.BlockSpec(memory_space=pltpu.VMEM)
    return pl.pallas_call(
        attend_kernel,
        out_shape=(
            jax.ShapeDtypeStruct((BIG_ROWS, BIG_LINE, 128), f32),
            jax.ShapeDtypeStruct((ROWS, LINE // 2, 128), bf16),
            jax.ShapeDtypeStruct((CARRIERS, 128), f32),
        ),
        in_specs=[pl.BlockSpec(memory_space=pltpu.SMEM), whole, whole, whole],
        out_specs=(whole, whole, whole),
        scratch_shapes=[
            pltpu.VMEM((BIG_ROWS, BIG_LINE, 128), f32),
            pltpu.VMEM((T_ROWS, T_LINE, 128), f32),
            pltpu.VMEM((4, ALL_KEYS, 128), f32),
            pltpu.VMEM((4, ALL_KEYS, 128), f32),
            pltpu.VMEM((4, ALL_KEYS, 256), bf16),
            pltpu.VMEM((CARRIERS, 256), bf16),
            pltpu.VMEM((CARRIERS, 256), f32),
        ],
        compiler_params=pltpu.CompilerParams(vmem_limit_bytes=40 * 2**20),
    )(place, big, qg, car)


def pair_heads(a, b):
    a = a.reshape(-1, HEADS, DIM)
    b = b.reshape(-1, HEADS, DIM)
    return jnp.concatenate([a, b], axis=-1).transpose(1, 0, 2)


def spread(x):
    return lax.all_to_all(x, RING, 0, 0, tiled=True)


def to_block(x):
    x = x.reshape(2, 2, 2, 8, 8, 4, 128)
    return x.transpose(0, 3, 1, 4, 2, 5, 6).reshape(ROWS, WIDE, TALL, 128)


def move(x, axis, step):
    n = lax.axis_size(axis)
    return lax.ppermute(x, axis, [(i, (i + step) % n) for i in range(n)])


def per_device(q, k, v, g, car_k, car_v, open_cells):
    f32, bf16 = jnp.float32, jnp.bfloat16
    solid = (open_cells < 1).reshape(1, 256, 1)
    solid = solid & (lax.broadcasted_iota(jnp.int32, (1, 1, 128), 2) < DIM)
    kv = jnp.where(solid, jnp.bfloat16(SOLID), pair_heads(k, v))
    car = jnp.concatenate(
        [c[:, h * DIM : h * DIM + DIM] for h in range(HEADS) for c in (car_k, car_v)], axis=1
    ).reshape(HEADS, 1, 128)
    car = jnp.concatenate([car, move(car, "z", -3), move(car, "z", 3)], axis=1)
    car = jnp.pad(car, ((0, 0), (0, 5), (0, 0)))
    qg = pair_heads(q * jnp.bfloat16(DIM**-0.5), g)
    kv = spread(jnp.concatenate([kv, qg, car], axis=1))
    own = to_block(kv[:, :256])
    car = kv[:, 512:515].transpose(1, 0, 2)
    qg = to_block(kv[:, 256:512])

    upper = move(jnp.concatenate([own[ROWS - REACH :], car[:, None]], axis=1), "z", 1)
    lower = move(jnp.concatenate([own[:REACH], car[:, None]], axis=1), "z", -1)
    big = jnp.concatenate([upper[:, :WIDE], own, lower[:, :WIDE]], axis=0)
    car = jnp.concatenate([car, lower[:, WIDE], upper[:2, WIDE]], axis=0)
    cells = BIG_ROWS * REACH
    left = big[:, WIDE - REACH :].reshape(cells, TALL, 128)
    right = big[:, :REACH].reshape(cells, TALL, 128)
    left = move(jnp.concatenate([left, car], axis=0), "x", 1)
    right = move(jnp.concatenate([right, car], axis=0), "x", -1)
    car = jnp.concatenate([car, left[cells:], right[cells:], move(car, "x", 2)], axis=0)
    shape = (BIG_ROWS, REACH, TALL, 128)
    big = jnp.concatenate([left[:cells].reshape(shape), big, right[:cells].reshape(shape)], axis=1)

    place = lax.axis_index("x").astype(jnp.int32).reshape(1)
    dbig, dq, dcar = attend(
        place,
        big.reshape(BIG_ROWS, BIG_LINE, 128),
        qg.reshape(ROWS, LINE, 128),
        car.reshape(CARRIERS, 128),
    )

    dbig = dbig.reshape(BIG_ROWS, WIDE + 2 * REACH, TALL, 128)
    dcar = dcar.reshape(4, 8, 8, 128)
    to_right = dbig[:, WIDE + REACH :].astype(bf16).reshape(cells, TALL, 128)
    to_left = dbig[:, :REACH].astype(bf16).reshape(cells, TALL, 128)
    low = dcar[1:].astype(bf16)
    from_left = move(jnp.concatenate([to_right, low[1]], axis=0), "x", 1).astype(f32)
    from_right = move(jnp.concatenate([to_left, low[0]], axis=0), "x", -1).astype(f32)
    dcar = dcar[0] + from_left[cells:] + from_right[cells:] + move(low[2], "x", 2).astype(f32)
    rest = WIDE - REACH
    mid = (
        dbig[:, REACH : WIDE + REACH]
        + jnp.pad(from_left[:cells].reshape(shape), ((0, 0), (0, rest), (0, 0), (0, 0)))
        + jnp.pad(from_right[:cells].reshape(shape), ((0, 0), (rest, 0), (0, 0), (0, 0)))
    )
    low = jnp.pad(dcar[3:].astype(bf16), ((0, 1), (0, 0), (0, 0)))
    to_down = jnp.concatenate([mid[ROWS + REACH :].astype(bf16), low[:3, None]], axis=1)
    to_up = jnp.concatenate([mid[:REACH].astype(bf16), low[3:, None]], axis=1)
    from_up = move(to_down, "z", 1).astype(f32)
    from_down = move(to_up, "z", -1).astype(f32)
    dcar = dcar[:3] + from_up[:, WIDE] + from_down[:, WIDE]
    rest = ROWS - REACH
    dkv = (
        mid[REACH : ROWS + REACH]
        + jnp.pad(from_up[:, :WIDE], ((0, rest), (0, 0), (0, 0), (0, 0)))
        + jnp.pad(from_down[:, :WIDE], ((rest, 0), (0, 0), (0, 0), (0, 0)))
    ).astype(bf16)

    dkv = dkv.reshape(2, 8, 2, 8, 2, 4, 128).transpose(0, 2, 4, 1, 3, 5, 6).reshape(8, 256, 128)
    dq = dq.reshape(2, 8, 2, 4, 2, 4, 128).transpose(0, 2, 4, 1, 3, 5, 6).reshape(8, 128, 128)
    dcar = jnp.pad(dcar.astype(bf16).transpose(1, 0, 2), ((0, 0), (0, 5), (0, 0)))
    back = spread(jnp.concatenate([dkv, dq, dcar], axis=1))
    dcar = back[:, 384:387].astype(f32)
    dcar = dcar[:, 0] + move(dcar[:, 1], "z", 3) + move(dcar[:, 2], "z", -3)
    dkv = back[:, :256].transpose(1, 0, 2)
    dq = back[:, 256:384].reshape(HEADS, 8, 4, 4, 2, DIM).transpose(1, 4, 2, 3, 0, 5)
    cells = (8, 8, 4, 512)
    return (
        dq.reshape(cells),
        dkv[..., :DIM].reshape(cells),
        dkv[..., DIM:].reshape(cells),
        dcar[:, :DIM].reshape(1, 512),
        dcar[:, DIM:].reshape(1, 512),
    )


def solution(mesh):
    fine = Mesh(mesh.devices.reshape(-1, 2, 4, 2, 2), ("z", "yh", "x", "yl", "core"))
    tokens = P(("z", "yh"), ("x", "yl"), "core", None)
    carriers = P(("z", "yh", "x", "yl", "core"), None)
    return jax.shard_map(
        per_device,
        mesh=fine,
        in_specs=(tokens, tokens, tokens, tokens, carriers, carriers, P(*tokens[:3])),
        out_specs=(tokens, tokens, tokens, carriers, carriers),
        check_vma=False,
    )
```

time: 145 us -> 107 us (0.74)
  starting transfers between devices: 55 us -> 28.3 us
  blocking collectives: 0 us -> 21.8 us
  waiting for transfers between devices: 46.8 us -> 29.6 us
  Pallas kernels: 24.4 us -> 11.2 us
  other arithmetic: 5.77 us -> 2.12 us
    all_to_all x0 -> x1, blocking collectives: none -> 21.8 us  [spread(): return lax.all_to_all(x, RING, 0, 0, tiled=True)]
    all_to_all x4 -> x1, starting transfers between devices: 26 us -> 5.42 us  [spread(): return lax.all_to_all(x, RING, 0, 0, tiled=True)]
    all_to_all x2 -> x0, waiting for transfers between devices: 17.6 us -> none  [the longest x1 9 us: per_device(): lax.all_to_all(dcar.reshape(nz * nx, 8, 128), ACROSS, 0, 0, tiled=True)]
    all_to_all x2 -> x0, starting transfers between devices: 13.3 us -> none  [the longest x1 8.85 us: per_device(): car = lax.all_to_all(car, ACROSS, 0, 0, tiled=True).reshape(CARRIERS, 128)]
    pallas_call x1, Pallas kernels: 24.4 us -> 11.2 us  [attend(): pl.pallas_call(attend_kernel, out_shape=(jax.ShapeDtypeStruct((BIG_ROWS,...]
    ppermute x8 -> x14, starting transfers between devices: 15.7 us -> 22.9 us  [move(): return lax.ppermute(x, axis, [(i, (i + step) % n) for i in range(n)])]
    ppermute x8 -> x14, waiting for transfers between devices: 7.41 us -> 14.3 us  [move(): return lax.ppermute(x, axis, [(i, (i + step) % n) for i in range(n)])]
    all_to_all x4 -> x1, waiting for transfers between devices: 21.8 us -> 15.3 us  [spread(): return lax.all_to_all(x, RING, 0, 0, tiled=True)]
  transfers between devices with their start and end apart: 14 -> 15, of which waited for: 8 -> 9; matrix products, arithmetic and copies ran while one was open for 5% -> 9% of each run, Pallas kernels for 0% -> 0%
where the time goes in v2:
time: 107 us
  waiting for transfers between devices  29.6 us (28%)
  starting transfers between devices  28.3 us (26%)
  blocking collectives  21.8 us (20%)
  local copies, waits for them, and re-layouts  12.7 us (12%)
  Pallas kernels  11.2 us (10%)
  other arithmetic  2.12 us (2%)
  between operations  1.17 us (1%)
    ppermute x14, starting transfers between devices, move(): return lax.ppermute(x, axis, [(i, (i + step) % n) for i in range(n)])  22.9 us
    all_to_all x1, blocking collectives, spread(): return lax.all_to_all(x, RING, 0, 0, tiled=True)  21.8 us
    all_to_all x1, waiting for transfers between devices, spread(): return lax.all_to_all(x, RING, 0, 0, tiled=True)  15.3 us
    ppermute x14, waiting for transfers between devices, move(): return lax.ppermute(x, axis, [(i, (i + step) % n) for i in range(n)])  14.3 us
    pallas_call x1, Pallas kernels, attend(): pl.pallas_call(attend_kernel, out_shape=(jax.ShapeDtypeStruct((BIG_ROWS,...  11.2 us
    all_to_all x1, starting transfers between devices, spread(): return lax.all_to_all(x, RING, 0, 0, tiled=True)  5.42 us
  transfers between devices with their start and end apart: 15, of which 9 were waited for; matrix products, arithmetic and copies ran while one was open for 9% of the time, Pallas kernels for 0%

profile of v2, /device:TPU:1, one launch (start us, length us, event | category | flops | bytes accessed | tf_op | source)
XLA Modules:
  0.0 106.9 jit_solution(5816356100818756731)
XLA Ops:
  0.7 0.9 fusion.29
  1.7 5.2 %collective-permute-start.1 = (bf16[8,1,128]{2,0,1:T(8,128)(2,1)S(1)}, bf16[8,1,128]{2,0,1:T(8,128)(2,1)S(1)}, u32[]{:S(2)}, u32[]{:S(2)}) collective-permute-start(bf16[8,1,128]{2,0,1:T(8,128)(2,1)S(1)} %bitcast.120), channel_id=1, source_target_pairs={{0,96},{32,128},{64,160},{96,192},{128,224},{160,0},{192,32},{224,... | collective-permute-start | bytes 6152 | tf_op jit(solution)/shard_map/ppermute | solution.py:219
  7.0 2.2 %collective-permute-start = (bf16[8,1,128]{2,0,1:T(8,128)(2,1)S(1)}, bf16[8,1,128]{2,0,1:T(8,128)(2,1)S(1)}, u32[]{:S(2)}, u32[]{:S(2)}) collective-permute-start(bf16[8,1,128]{2,0,1:T(8,128)(2,1)S(1)} %bitcast.121), channel_id=1, source_target_pairs={{0,160},{32,192},{64,224},{96,0},{128,32},{160,64},{192,96},{224,1... | collective-permute-start | bytes 6152 | tf_op jit(solution)/shard_map/ppermute | solution.py:219
  9.2 1.3 %reshape.153 = bf16[256,8,64]{2,1,0:T(8,128)(2,1)S(1)} reshape(bf16[8,8,4,512]{3,2,1,0:T(4,128)(2,1)} %param.9) | data formatting | bytes 524288 | tf_op jit(solution)/shard_map/reshape | solution.py:204
  10.5 1.3 %reshape.152 = bf16[256,8,64]{2,1,0:T(8,128)(2,1)S(1)} reshape(bf16[8,8,4,512]{3,2,1,0:T(4,128)(2,1)} %param.8) | data formatting | bytes 524288 | tf_op jit(solution)/shard_map/reshape | solution.py:203
  12.0 0.3 reshape.155
  12.4 0.3 reshape.154
  12.8 0.7 fusion.5
  13.7 1.1 %copy.57 = bf16[8,520,128]{2,1,0:T(8,128)(2,1)} copy(bf16[8,520,128]{2,0,1:T(8,128)(2,1)S(1)} %pad_maximum_fusion) | data formatting | bytes 2129920 | tf_op jit(solution)/shard_map/concatenate | solution.py:233
  14.9 5.4 %all-to-all-start = ((bf16[8,520,128]{2,1,0:T(8,128)(2,1)}), bf16[8,520,128]{2,1,0:T(8,128)(2,1)S(1)}, u32[]{:S(2)}, u32[]{:S(2)}) async-start(bf16[8,520,128]{2,1,0:T(8,128)(2,1)} %copy.57), calls=%async_computation | async-start | bytes 2129920 | tf_op jit(solution)/shard_map/all_to_all | solution.py:209
  20.3 15.3 %all-to-all-done = bf16[8,520,128]{2,1,0:T(8,128)(2,1)S(1)} async-done(((bf16[8,520,128]{2,1,0:T(8,128)(2,1)}), bf16[8,520,128]{2,1,0:T(8,128)(2,1)S(1)}, u32[]{:S(2)}, u32[]{:S(2)}) %all-to-all-start) | async-done | bytes 1064992 | tf_op jit(solution)/shard_map/all_to_all | solution.py:209
  35.7 0.3 copy.58
  36.0 2.6 %collective-permute-start.3 = (bf16[3,17,8,128]{3,2,0,1:T(8,128)(2,1)S(1)}, bf16[3,17,8,128]{3,2,0,1:T(8,128)(2,1)S(1)}, u32[]{:S(2)}, u32[]{:S(2)}) collective-permute-start(bf16[3,17,8,128]{3,2,0,1:T(8,128)(2,1)S(1)} %get-tuple-element.36), channel_id=1, source_target_pairs={{0,224},{32,0},{64,32},{96,64},{128,96},{160,128},{192,160},{224,1... | collective-permute-start | bytes 313352 | tf_op jit(solution)/shard_map/ppermute | solution.py:219
  38.6 0.4 collective-permute-start.2
  39.0 0.3 copy.65
  39.3 2.1 %collective-permute-done.3 = bf16[3,17,8,128]{3,2,0,1:T(8,128)(2,1)S(1)} collective-permute-done((bf16[3,17,8,128]{3,2,0,1:T(8,128)(2,1)S(1)}, bf16[3,17,8,128]{3,2,0,1:T(8,128)(2,1)S(1)}, u32[]{:S(2)}, u32[]{:S(2)}) %collective-permute-start.3) | collective-permute-done | bytes 104480 | tf_op jit(solution)/shard_map/ppermute | solution.py:219
  41.4 2.0 %collective-permute-done.2 = bf16[3,17,8,128]{3,2,0,1:T(8,128)(2,1)S(1)} collective-permute-done((bf16[3,17,8,128]{3,2,0,1:T(8,128)(2,1)S(1)}, bf16[3,17,8,128]{3,2,0,1:T(8,128)(2,1)S(1)}, u32[]{:S(2)}, u32[]{:S(2)}) %collective-permute-start.2) | collective-permute-done | bytes 104480 | tf_op jit(solution)/shard_map/ppermute | solution.py:219
  43.6 1.3 %collective-permute-start.4 = (bf16[74,8,128]{2,1,0:T(8,128)(2,1)S(1)}, bf16[74,8,128]{2,1,0:T(8,128)(2,1)S(1)}, u32[]{:S(2)}, u32[]{:S(2)}) collective-permute-start(bf16[74,8,128]{2,1,0:T(8,128)(2,1)S(1)} %get-tuple-element.32), channel_id=1, source_target_pairs={{0,4},{4,8},{8,12},{12,0},{1,5},{5,9},{9,13},{13,1},{2,6},{6,10},{... | collective-permute-start | bytes 454664 | tf_op jit(solution)/shard_map/ppermute | solution.py:219
  44.9 1.5 %collective-permute-start.5 = (bf16[74,8,128]{2,1,0:T(8,128)(2,1)S(1)}, bf16[74,8,128]{2,1,0:T(8,128)(2,1)S(1)}, u32[]{:S(2)}, u32[]{:S(2)}) collective-permute-start(bf16[74,8,128]{2,1,0:T(8,128)(2,1)S(1)} %get-tuple-element.33), channel_id=1, source_target_pairs={{0,12},{4,0},{8,4},{12,8},{1,13},{5,1},{9,5},{13,9},{2,14},{6,2},{... | collective-permute-start | bytes 454664 | tf_op jit(solution)/shard_map/ppermute | solution.py:219
  46.4 1.5 %collective-permute-start.6 = (bf16[8,8,128]{2,1,0:T(8,128)(2,1)S(1)}, bf16[8,8,128]{2,1,0:T(8,128)(2,1)S(1)}, u32[]{:S(2)}, u32[]{:S(2)}) collective-permute-start(bf16[8,8,128]{2,1,0:T(8,128)(2,1)S(1)} %pad_maximum_fusion.17), channel_id=1, source_target_pairs={{0,8},{4,12},{8,0},{12,4},{1,9},{5,13},{9,1},{13,5},{2,10},{6,14},... | collective-permute-start | bytes 49160 | tf_op jit(solution)/shard_map/ppermute | solution.py:219
  47.9 1.0 collective-permute-done.4
  49.0 0.2 copy_bitcast_fusion.big
  49.2 1.4 %collective-permute-done.6 = bf16[8,8,128]{2,1,0:T(8,128)(2,1)S(1)} collective-permute-done((bf16[8,8,128]{2,1,0:T(8,128)(2,1)S(1)}, bf16[8,8,128]{2,1,0:T(8,128)(2,1)S(1)}, u32[]{:S(2)}, u32[]{:S(2)}) %collective-permute-start.6) | collective-permute-done | bytes 16416 | tf_op jit(solution)/shard_map/ppermute | solution.py:219
  50.6 11.2 %shard_map.110 = (f32[22,176,128]{2,1,0:T(8,128)S(1)}, bf16[16,64,128]{2,1,0:T(8,128)(2,1)S(1)}, f32[256,128]{1,0:T(8,128)S(1)}) custom-call(s32[1]{0:T(128)} %bitcast.place, bf16[22,176,128]{2,1,0:T(8,128)(2,1)S(1)} %copy_bitcast_fusion.big, bf16[16,128,128]{2,1,0:T(8,128)(2,1)S(1)} %bitcast.99, bf16[256,128]{1,0:T(8,128)(2,1)S(1)} %bitcast.101), custom_call_target="tpu_custom_call" | custom-call | tf_op jit(solution)/shard_map/pallas_call | solution.py:180
  62.0 1.3 %collective-permute-start.8 = (bf16[74,8,128]{2,1,0:T(8,128)(2,1)S(1)}, bf16[74,8,128]{2,1,0:T(8,128)(2,1)S(1)}, u32[]{:S(2)}, u32[]{:S(2)}) collective-permute-start(bf16[74,8,128]{2,1,0:T(8,128)(2,1)S(1)} %pad_maximum_fusion.9), channel_id=1, source_target_pairs={{0,12},{4,0},{8,4},{12,8},{1,13},{5,1},{9,5},{13,9},{2,14},{6,2},{... | collective-permute-start | bytes 454664 | tf_op jit(solution)/shard_map/ppermute | solution.py:219
  63.4 0.3 collective-permute-start.7
  63.6 1.6 %collective-permute-start.9 = (bf16[8,8,128]{2,1,0:T(8,128)(2,1)S(1)}, bf16[8,8,128]{2,1,0:T(8,128)(2,1)S(1)}, u32[]{:S(2)}, u32[]{:S(2)}) collective-permute-start(bf16[8,8,128]{2,1,0:T(8,128)(2,1)S(1)} %get-tuple-element.30), channel_id=1, source_target_pairs={{0,8},{4,12},{8,0},{12,4},{1,9},{5,13},{9,1},{13,5},{2,10},{6,14},... | collective-permute-start | bytes 49160 | tf_op jit(solution)/shard_map/ppermute | solution.py:219
  65.2 0.9 collective-permute-done.8
  66.1 2.7 %collective-permute-done.7 = bf16[74,8,128]{2,1,0:T(8,128)(2,1)S(1)} collective-permute-done((bf16[74,8,128]{2,1,0:T(8,128)(2,1)S(1)}, bf16[74,8,128]{2,1,0:T(8,128)(2,1)S(1)}, u32[]{:S(2)}, u32[]{:S(2)}) %collective-permute-start.7) | collective-permute-done | bytes 151584 | tf_op jit(solution)/shard_map/ppermute | solution.py:219
  69.0 0.3 fusion.19
  69.3 1.1 %collective-permute-start.11 = (bf16[3,17,8,128]{3,2,1,0:T(8,128)(2,1)S(1)}, bf16[3,17,8,128]{3,2,1,0:T(8,128)(2,1)S(1)}, u32[]{:S(2)}, u32[]{:S(2)}) collective-permute-start(bf16[3,17,8,128]{3,2,1,0:T(8,128)(2,1)S(1)} %pad_maximum_fusion.16), channel_id=1, source_target_pairs={{0,224},{32,0},{64,32},{96,64},{128,96},{160,128},{192,160},{224,1... | collective-permute-start | bytes 313352 | tf_op jit(solution)/shard_map/ppermute | solution.py:219
  70.4 0.5 collective-permute-start.10
  71.1 2.2 %collective-permute-done.11 = bf16[3,17,8,128]{3,2,1,0:T(8,128)(2,1)S(1)} collective-permute-done((bf16[3,17,8,128]{3,2,1,0:T(8,128)(2,1)S(1)}, bf16[3,17,8,128]{3,2,1,0:T(8,128)(2,1)S(1)}, u32[]{:S(2)}, u32[]{:S(2)}) %collective-permute-start.11) | collective-permute-done | bytes 104480 | tf_op jit(solution)/shard_map/ppermute | solution.py:219
  73.2 2.0 %collective-permute-done.10 = bf16[3,17,8,128]{3,2,0,1:T(8,128)(2,1)S(1)} collective-permute-done((bf16[3,17,8,128]{3,2,0,1:T(8,128)(2,1)S(1)}, bf16[3,17,8,128]{3,2,0,1:T(8,128)(2,1)S(1)}, u32[]{:S(2)}, u32[]{:S(2)}) %collective-permute-start.10) | collective-permute-done | bytes 104480 | tf_op jit(solution)/shard_map/ppermute | solution.py:219
  75.5 0.2 copy.70
  75.7 21.8 %all_to_all.10 = bf16[8,392,128]{2,1,0:T(8,128)(2,1)S(1)} all-to-all(bf16[8,392,128]{2,1,0:T(8,128)(2,1)S(1)} %fusion.4), channel_id=1, replica_groups=mesh['z'=8,'yh'=2,'x'=4,'yl'=2,'core'=2] {'yh','yl','core'}, dimensions={0} | all-to-all | bytes 1605632 | tf_op jit(solution)/shard_map/all_to_all | solution.py:209
  97.6 2.0 %collective-permute-start.13 = (f32[8,128]{1,0:T(8,128)S(1)}, f32[8,128]{1,0:T(8,128)S(1)}, u32[]{:S(2)}, u32[]{:S(2)}) collective-permute-start(f32[8,128]{1,0:T(8,128)S(1)} %get-tuple-element.35), channel_id=1, source_target_pairs={{0,160},{32,192},{64,224},{96,0},{128,32},{160,64},{192,96},{224,1... | collective-permute-start | bytes 12296 | tf_op jit(solution)/shard_map/ppermute | solution.py:219
  99.6 1.4 %collective-permute-start.12 = (f32[8,128]{1,0:T(8,128)S(1)}, f32[8,128]{1,0:T(8,128)S(1)}, u32[]{:S(2)}, u32[]{:S(2)}) collective-permute-start(f32[8,128]{1,0:T(8,128)S(1)} %get-tuple-element.34), channel_id=1, source_target_pairs={{0,96},{32,128},{64,160},{96,192},{128,224},{160,0},{192,32},{224,... | collective-permute-start | bytes 12296 | tf_op jit(solution)/shard_map/ppermute | solution.py:219
  101.0 0.2 fusion.26
  101.2 0.2 reshape.175
  101.5 0.3 copy.73
  101.8 1.0 reshape.176
  102.8 0.3 copy.74
  103.2 1.0 reshape.177
  104.2 0.3 copy.75
  104.5 1.0 reshape.178
  105.6 0.7 reshape.179
  106.3 0.7 reshape.180
  (76 shorter events, 2.0 us)
Async XLA Ops:
  0.6 11.1 %copy-start.2 = (s32[8,8,4]{1,2,0:T(4,128)S(1)}, s32[8,8,4]{1,2,0:T(4,128)}, u32[]{:S(2)}) copy-start(s32[8,8,4]{1,2,0:T(4,128)} %param.13) | copy-start | bytes 3076
  0.6 11.4 %copy-start = (bf16[8,8,4,512]{3,2,1,0:T(4,128)(2,1)S(1)}, bf16[8,8,4,512]{3,2,1,0:T(4,128)(2,1)}, u32[]{:S(2)}) copy-start(bf16[8,8,4,512]{3,2,1,0:T(4,128)(2,1)} %param.10) | copy-start | bytes 786436
  0.7 11.7 %copy-start.1 = (bf16[8,8,4,512]{3,2,1,0:T(4,128)(2,1)S(1)}, bf16[8,8,4,512]{3,2,1,0:T(4,128)(2,1)}, u32[]{:S(2)}) copy-start(bf16[8,8,4,512]{3,2,1,0:T(4,128)(2,1)} %param.7) | copy-start | bytes 786436
  1.7 11.8 %collective-permute-start.1 = (bf16[8,1,128]{2,0,1:T(8,128)(2,1)S(1)}, bf16[8,1,128]{2,0,1:T(8,128)(2,1)S(1)}, u32[]{:S(2)}, u32[]{:S(2)}) collective-permute-start(bf16[8,1,128]{2,0,1:T(8,128)(2,1)S(1)} %bitcast.120), channel_id=1, source_target_pairs={{0,96},{32,128},{64,160},{96,192},{128,224},{160,0},{192,32},{224,... | collective-permute-start | bytes 6152 | tf_op jit(solution)/shard_map/ppermute | solution.py:219
  7.0 6.6 %collective-permute-start = (bf16[8,1,128]{2,0,1:T(8,128)(2,1)S(1)}, bf16[8,1,128]{2,0,1:T(8,128)(2,1)S(1)}, u32[]{:S(2)}, u32[]{:S(2)}) collective-permute-start(bf16[8,1,128]{2,0,1:T(8,128)(2,1)S(1)} %bitcast.121), channel_id=1, source_target_pairs={{0,160},{32,192},{64,224},{96,0},{128,32},{160,64},{192,96},{224,1... | collective-permute-start | bytes 6152 | tf_op jit(solution)/shard_map/ppermute | solution.py:219
  14.9 20.7 %all-to-all-start = ((bf16[8,520,128]{2,1,0:T(8,128)(2,1)}), bf16[8,520,128]{2,1,0:T(8,128)(2,1)S(1)}, u32[]{:S(2)}, u32[]{:S(2)}) async-start(bf16[8,520,128]{2,1,0:T(8,128)(2,1)} %copy.57), calls=%async_computation | async-start | bytes 2129920 | tf_op jit(solution)/shard_map/all_to_all | solution.py:209
  36.0 5.3 %collective-permute-start.3 = (bf16[3,17,8,128]{3,2,0,1:T(8,128)(2,1)S(1)}, bf16[3,17,8,128]{3,2,0,1:T(8,128)(2,1)S(1)}, u32[]{:S(2)}, u32[]{:S(2)}) collective-permute-start(bf16[3,17,8,128]{3,2,0,1:T(8,128)(2,1)S(1)} %get-tuple-element.36), channel_id=1, source_target_pairs={{0,224},{32,0},{64,32},{96,64},{128,96},{160,128},{192,160},{224,1... | collective-permute-start | bytes 313352 | tf_op jit(solution)/shard_map/ppermute | solution.py:219
  38.6 4.7 %collective-permute-start.2 = (bf16[3,17,8,128]{3,2,0,1:T(8,128)(2,1)S(1)}, bf16[3,17,8,128]{3,2,0,1:T(8,128)(2,1)S(1)}, u32[]{:S(2)}, u32[]{:S(2)}) collective-permute-start(bf16[3,17,8,128]{3,2,0,1:T(8,128)(2,1)S(1)} %get-tuple-element.37), channel_id=1, source_target_pairs={{0,32},{32,64},{64,96},{96,128},{128,160},{160,192},{192,224},{224... | collective-permute-start | bytes 313352 | tf_op jit(solution)/shard_map/ppermute | solution.py:219
  43.6 5.3 %collective-permute-start.4 = (bf16[74,8,128]{2,1,0:T(8,128)(2,1)S(1)}, bf16[74,8,128]{2,1,0:T(8,128)(2,1)S(1)}, u32[]{:S(2)}, u32[]{:S(2)}) collective-permute-start(bf16[74,8,128]{2,1,0:T(8,128)(2,1)S(1)} %get-tuple-element.32), channel_id=1, source_target_pairs={{0,4},{4,8},{8,12},{12,0},{1,5},{5,9},{9,13},{13,1},{2,6},{6,10},{... | collective-permute-start | bytes 454664 | tf_op jit(solution)/shard_map/ppermute | solution.py:219
  44.9 4.1 %collective-permute-start.5 = (bf16[74,8,128]{2,1,0:T(8,128)(2,1)S(1)}, bf16[74,8,128]{2,1,0:T(8,128)(2,1)S(1)}, u32[]{:S(2)}, u32[]{:S(2)}) collective-permute-start(bf16[74,8,128]{2,1,0:T(8,128)(2,1)S(1)} %get-tuple-element.33), channel_id=1, source_target_pairs={{0,12},{4,0},{8,4},{12,8},{1,13},{5,1},{9,5},{13,9},{2,14},{6,2},{... | collective-permute-start | bytes 454664 | tf_op jit(solution)/shard_map/ppermute | solution.py:219
  46.4 4.2 %collective-permute-start.6 = (bf16[8,8,128]{2,1,0:T(8,128)(2,1)S(1)}, bf16[8,8,128]{2,1,0:T(8,128)(2,1)S(1)}, u32[]{:S(2)}, u32[]{:S(2)}) collective-permute-start(bf16[8,8,128]{2,1,0:T(8,128)(2,1)S(1)} %pad_maximum_fusion.17), channel_id=1, source_target_pairs={{0,8},{4,12},{8,0},{12,4},{1,9},{5,13},{9,1},{13,5},{2,10},{6,14},... | collective-permute-start | bytes 49160 | tf_op jit(solution)/shard_map/ppermute | solution.py:219
  62.0 4.1 %collective-permute-start.8 = (bf16[74,8,128]{2,1,0:T(8,128)(2,1)S(1)}, bf16[74,8,128]{2,1,0:T(8,128)(2,1)S(1)}, u32[]{:S(2)}, u32[]{:S(2)}) collective-permute-start(bf16[74,8,128]{2,1,0:T(8,128)(2,1)S(1)} %pad_maximum_fusion.9), channel_id=1, source_target_pairs={{0,12},{4,0},{8,4},{12,8},{1,13},{5,1},{9,5},{13,9},{2,14},{6,2},{... | collective-permute-start | bytes 454664 | tf_op jit(solution)/shard_map/ppermute | solution.py:219
  63.4 5.5 %collective-permute-start.7 = (bf16[74,8,128]{2,1,0:T(8,128)(2,1)S(1)}, bf16[74,8,128]{2,1,0:T(8,128)(2,1)S(1)}, u32[]{:S(2)}, u32[]{:S(2)}) collective-permute-start(bf16[74,8,128]{2,1,0:T(8,128)(2,1)S(1)} %pad_maximum_fusion.8), channel_id=1, source_target_pairs={{0,4},{4,8},{8,12},{12,0},{1,5},{5,9},{9,13},{13,1},{2,6},{6,10},{... | collective-permute-start | bytes 454664 | tf_op jit(solution)/shard_map/ppermute | solution.py:219
  63.6 5.3 %collective-permute-start.9 = (bf16[8,8,128]{2,1,0:T(8,128)(2,1)S(1)}, bf16[8,8,128]{2,1,0:T(8,128)(2,1)S(1)}, u32[]{:S(2)}, u32[]{:S(2)}) collective-permute-start(bf16[8,8,128]{2,1,0:T(8,128)(2,1)S(1)} %get-tuple-element.30), channel_id=1, source_target_pairs={{0,8},{4,12},{8,0},{12,4},{1,9},{5,13},{9,1},{13,5},{2,10},{6,14},... | collective-permute-start | bytes 49160 | tf_op jit(solution)/shard_map/ppermute | solution.py:219
  69.3 3.9 %collective-permute-start.11 = (bf16[3,17,8,128]{3,2,1,0:T(8,128)(2,1)S(1)}, bf16[3,17,8,128]{3,2,1,0:T(8,128)(2,1)S(1)}, u32[]{:S(2)}, u32[]{:S(2)}) collective-permute-start(bf16[3,17,8,128]{3,2,1,0:T(8,128)(2,1)S(1)} %pad_maximum_fusion.16), channel_id=1, source_target_pairs={{0,224},{32,0},{64,32},{96,64},{128,96},{160,128},{192,160},{224,1... | collective-permute-start | bytes 313352 | tf_op jit(solution)/shard_map/ppermute | solution.py:219
  70.4 4.8 %collective-permute-start.10 = (bf16[3,17,8,128]{3,2,0,1:T(8,128)(2,1)S(1)}, bf16[3,17,8,128]{3,2,0,1:T(8,128)(2,1)S(1)}, u32[]{:S(2)}, u32[]{:S(2)}) collective-permute-start(bf16[3,17,8,128]{3,2,0,1:T(8,128)(2,1)S(1)} %pad_maximum_fusion.15), channel_id=1, source_target_pairs={{0,32},{32,64},{64,96},{96,128},{128,160},{160,192},{192,224},{224... | collective-permute-start | bytes 313352 | tf_op jit(solution)/shard_map/ppermute | solution.py:219
  97.6 8.0 %collective-permute-start.13 = (f32[8,128]{1,0:T(8,128)S(1)}, f32[8,128]{1,0:T(8,128)S(1)}, u32[]{:S(2)}, u32[]{:S(2)}) collective-permute-start(f32[8,128]{1,0:T(8,128)S(1)} %get-tuple-element.35), channel_id=1, source_target_pairs={{0,160},{32,192},{64,224},{96,0},{128,32},{160,64},{192,96},{224,1... | collective-permute-start | bytes 12296 | tf_op jit(solution)/shard_map/ppermute | solution.py:219
  99.6 6.0 %collective-permute-start.12 = (f32[8,128]{1,0:T(8,128)S(1)}, f32[8,128]{1,0:T(8,128)S(1)}, u32[]{:S(2)}, u32[]{:S(2)}) collective-permute-start(f32[8,128]{1,0:T(8,128)S(1)} %get-tuple-element.34), channel_id=1, source_target_pairs={{0,96},{32,128},{64,160},{96,192},{128,224},{160,0},{192,32},{224,... | collective-permute-start | bytes 12296 | tf_op jit(solution)/shard_map/ppermute | solution.py:219

commit v3 on v2

--- a/solution.py
+++ b/solution.py
@@ -287,8 +287,15 @@
     dq = dq.reshape(2, 8, 2, 4, 2, 4, 128).transpose(0, 2, 4, 1, 3, 5, 6).reshape(8, 128, 128)
     dcar = jnp.pad(dcar.astype(bf16).transpose(1, 0, 2), ((0, 0), (0, 5), (0, 0)))
     back = spread(jnp.concatenate([dkv, dq, dcar], axis=1))
-    dcar = back[:, 384:387].astype(f32)
-    dcar = dcar[:, 0] + move(dcar[:, 1], "z", 3) + move(dcar[:, 2], "z", -3)
+    dcar = back[:, 384:387]
+    dcar = jnp.concatenate(
+        [dcar[h, :, d : d + DIM] for d in (0, DIM) for h in range(HEADS)], axis=1
+    )
+    dcar = (
+        dcar[:1].astype(f32)
+        + move(dcar[1:2], "z", 3).astype(f32)
+        + move(dcar[2:], "z", -3).astype(f32)
+    )
     dkv = back[:, :256].transpose(1, 0, 2)
     dq = back[:, 256:384].reshape(HEADS, 8, 4, 4, 2, DIM).transpose(1, 4, 2, 3, 0, 5)
     cells = (8, 8, 4, 512)
@@ -296,8 +303,8 @@
         dq.reshape(cells),
         dkv[..., :DIM].reshape(cells),
         dkv[..., DIM:].reshape(cells),
-        dcar[:, :DIM].reshape(1, 512),
-        dcar[:, DIM:].reshape(1, 512),
+        dcar[:, :512],
+        dcar[:, 512:],
     )
 
 

time: 107 us -> 107 us (level)
    reshape x3 -> x0, local copies, waits for them, and re-layouts: 1.4 us -> none  [the longest x1 0.65 us: per_device(): dcar[:, :DIM].reshape(1, 512)]
where the time goes in v3:
time: 107 us; the launch traced here: 106 us
  waiting for transfers between devices  29.6 us (28%)
  starting transfers between devices  28.4 us (27%)
  blocking collectives  21.8 us (20%)
  local copies, waits for them, and re-layouts  12.1 us (11%)
  Pallas kernels  11.2 us (10%)
  other arithmetic  2.08 us (2%)
  between operations  1.17 us (1%)
    ppermute x14, starting transfers between devices, move(): return lax.ppermute(x, axis, [(i, (i + step) % n) for i in range(n)])  22.9 us
    all_to_all x1, blocking collectives, spread(): return lax.all_to_all(x, RING, 0, 0, tiled=True)  21.8 us
    all_to_all x1, waiting for transfers between devices, spread(): return lax.all_to_all(x, RING, 0, 0, tiled=True)  15.3 us
    ppermute x14, waiting for transfers between devices, move(): return lax.ppermute(x, axis, [(i, (i + step) % n) for i in range(n)])  14.3 us
    pallas_call x1, Pallas kernels, attend(): pl.pallas_call(attend_kernel, out_shape=(jax.ShapeDtypeStruct((BIG_ROWS,...  11.2 us
    all_to_all x1, starting transfers between devices, spread(): return lax.all_to_all(x, RING, 0, 0, tiled=True)  5.42 us
  transfers between devices with their start and end apart: 15, of which 9 were waited for; matrix products, arithmetic and copies ran while one was open for 9% of the time, Pallas kernels for 0%

profile of v3, /device:TPU:1, one launch (start us, length us, event | category | flops | bytes accessed | tf_op | source)
XLA Modules:
  0.0 106.3 jit_solution(12800085335076060795)
XLA Ops:
  0.7 0.9 fusion.30
  1.7 5.2 %collective-permute-start.1 = (bf16[8,1,128]{2,0,1:T(8,128)(2,1)S(1)}, bf16[8,1,128]{2,0,1:T(8,128)(2,1)S(1)}, u32[]{:S(2)}, u32[]{:S(2)}) collective-permute-start(bf16[8,1,128]{2,0,1:T(8,128)(2,1)S(1)} %bitcast.140), channel_id=1, source_target_pairs={{0,96},{32,128},{64,160},{96,192},{128,224},{160,0},{192,32},{224,... | collective-permute-start | bytes 6152 | tf_op jit(solution)/shard_map/ppermute | solution.py:219
  7.0 2.2 %collective-permute-start = (bf16[8,1,128]{2,0,1:T(8,128)(2,1)S(1)}, bf16[8,1,128]{2,0,1:T(8,128)(2,1)S(1)}, u32[]{:S(2)}, u32[]{:S(2)}) collective-permute-start(bf16[8,1,128]{2,0,1:T(8,128)(2,1)S(1)} %bitcast.141), channel_id=1, source_target_pairs={{0,160},{32,192},{64,224},{96,0},{128,32},{160,64},{192,96},{224,1... | collective-permute-start | bytes 6152 | tf_op jit(solution)/shard_map/ppermute | solution.py:219
  9.2 1.3 %reshape.147 = bf16[256,8,64]{2,1,0:T(8,128)(2,1)S(1)} reshape(bf16[8,8,4,512]{3,2,1,0:T(4,128)(2,1)} %param.9) | data formatting | bytes 524288 | tf_op jit(solution)/shard_map/reshape | solution.py:204
  10.5 1.3 %reshape.146 = bf16[256,8,64]{2,1,0:T(8,128)(2,1)S(1)} reshape(bf16[8,8,4,512]{3,2,1,0:T(4,128)(2,1)} %param.8) | data formatting | bytes 524288 | tf_op jit(solution)/shard_map/reshape | solution.py:203
  12.0 0.3 reshape.149
  12.4 0.3 reshape.148
  12.8 0.7 fusion.5
  13.6 0.1 pad_maximum_fusion
  13.7 1.1 %copy.45 = bf16[8,520,128]{2,1,0:T(8,128)(2,1)} copy(bf16[8,520,128]{2,0,1:T(8,128)(2,1)S(1)} %pad_maximum_fusion) | data formatting | bytes 2129920 | tf_op jit(solution)/shard_map/concatenate | solution.py:233
  14.8 5.4 %all-to-all-start = ((bf16[8,520,128]{2,1,0:T(8,128)(2,1)}), bf16[8,520,128]{2,1,0:T(8,128)(2,1)S(1)}, u32[]{:S(2)}, u32[]{:S(2)}) async-start(bf16[8,520,128]{2,1,0:T(8,128)(2,1)} %copy.45), calls=%async_computation | async-start | bytes 2129920 | tf_op jit(solution)/shard_map/all_to_all | solution.py:209
  20.3 15.3 %all-to-all-done = bf16[8,520,128]{2,1,0:T(8,128)(2,1)S(1)} async-done(((bf16[8,520,128]{2,1,0:T(8,128)(2,1)}), bf16[8,520,128]{2,1,0:T(8,128)(2,1)S(1)}, u32[]{:S(2)}, u32[]{:S(2)}) %all-to-all-start) | async-done | bytes 1064992 | tf_op jit(solution)/shard_map/all_to_all | solution.py:209
  35.7 0.3 copy.46
  36.0 2.6 %collective-permute-start.3 = (bf16[3,17,8,128]{3,2,0,1:T(8,128)(2,1)S(1)}, bf16[3,17,8,128]{3,2,0,1:T(8,128)(2,1)S(1)}, u32[]{:S(2)}, u32[]{:S(2)}) collective-permute-start(bf16[3,17,8,128]{3,2,0,1:T(8,128)(2,1)S(1)} %get-tuple-element.52), channel_id=1, source_target_pairs={{0,224},{32,0},{64,32},{96,64},{128,96},{160,128},{192,160},{224,1... | collective-permute-start | bytes 313352 | tf_op jit(solution)/shard_map/ppermute | solution.py:219
  38.6 0.4 collective-permute-start.2
  39.0 0.3 copy.53
  39.3 2.1 %collective-permute-done.3 = bf16[3,17,8,128]{3,2,0,1:T(8,128)(2,1)S(1)} collective-permute-done((bf16[3,17,8,128]{3,2,0,1:T(8,128)(2,1)S(1)}, bf16[3,17,8,128]{3,2,0,1:T(8,128)(2,1)S(1)}, u32[]{:S(2)}, u32[]{:S(2)}) %collective-permute-start.3) | collective-permute-done | bytes 104480 | tf_op jit(solution)/shard_map/ppermute | solution.py:219
  41.4 2.0 %collective-permute-done.2 = bf16[3,17,8,128]{3,2,0,1:T(8,128)(2,1)S(1)} collective-permute-done((bf16[3,17,8,128]{3,2,0,1:T(8,128)(2,1)S(1)}, bf16[3,17,8,128]{3,2,0,1:T(8,128)(2,1)S(1)}, u32[]{:S(2)}, u32[]{:S(2)}) %collective-permute-start.2) | collective-permute-done | bytes 104480 | tf_op jit(solution)/shard_map/ppermute | solution.py:219
  43.6 1.3 %collective-permute-start.4 = (bf16[74,8,128]{2,1,0:T(8,128)(2,1)S(1)}, bf16[74,8,128]{2,1,0:T(8,128)(2,1)S(1)}, u32[]{:S(2)}, u32[]{:S(2)}) collective-permute-start(bf16[74,8,128]{2,1,0:T(8,128)(2,1)S(1)} %get-tuple-element.48), channel_id=1, source_target_pairs={{0,4},{4,8},{8,12},{12,0},{1,5},{5,9},{9,13},{13,1},{2,6},{6,10},{... | collective-permute-start | bytes 454664 | tf_op jit(solution)/shard_map/ppermute | solution.py:219
  44.9 1.5 %collective-permute-start.5 = (bf16[74,8,128]{2,1,0:T(8,128)(2,1)S(1)}, bf16[74,8,128]{2,1,0:T(8,128)(2,1)S(1)}, u32[]{:S(2)}, u32[]{:S(2)}) collective-permute-start(bf16[74,8,128]{2,1,0:T(8,128)(2,1)S(1)} %get-tuple-element.49), channel_id=1, source_target_pairs={{0,12},{4,0},{8,4},{12,8},{1,13},{5,1},{9,5},{13,9},{2,14},{6,2},{... | collective-permute-start | bytes 454664 | tf_op jit(solution)/shard_map/ppermute | solution.py:219
  46.4 1.5 %collective-permute-start.6 = (bf16[8,8,128]{2,1,0:T(8,128)(2,1)S(1)}, bf16[8,8,128]{2,1,0:T(8,128)(2,1)S(1)}, u32[]{:S(2)}, u32[]{:S(2)}) collective-permute-start(bf16[8,8,128]{2,1,0:T(8,128)(2,1)S(1)} %pad_maximum_fusion.17), channel_id=1, source_target_pairs={{0,8},{4,12},{8,0},{12,4},{1,9},{5,13},{9,1},{13,5},{2,10},{6,14},... | collective-permute-start | bytes 49160 | tf_op jit(solution)/shard_map/ppermute | solution.py:219
  47.9 1.0 collective-permute-done.4
  49.0 0.2 copy_bitcast_fusion.big
  49.2 1.4 %collective-permute-done.6 = bf16[8,8,128]{2,1,0:T(8,128)(2,1)S(1)} collective-permute-done((bf16[8,8,128]{2,1,0:T(8,128)(2,1)S(1)}, bf16[8,8,128]{2,1,0:T(8,128)(2,1)S(1)}, u32[]{:S(2)}, u32[]{:S(2)}) %collective-permute-start.6) | collective-permute-done | bytes 16416 | tf_op jit(solution)/shard_map/ppermute | solution.py:219
  50.6 11.2 %shard_map.110 = (f32[22,176,128]{2,1,0:T(8,128)S(1)}, bf16[16,64,128]{2,1,0:T(8,128)(2,1)S(1)}, f32[256,128]{1,0:T(8,128)S(1)}) custom-call(s32[1]{0:T(128)} %bitcast.place, bf16[22,176,128]{2,1,0:T(8,128)(2,1)S(1)} %copy_bitcast_fusion.big, bf16[16,128,128]{2,1,0:T(8,128)(2,1)S(1)} %bitcast.119, bf16[256,128]{1,0:T(8,128)(2,1)S(1)} %bitcast.121), custom_call_target="tpu_custom_call" | custom-call | tf_op jit(solution)/shard_map/pallas_call | solution.py:180
  62.0 1.3 %collective-permute-start.8 = (bf16[74,8,128]{2,1,0:T(8,128)(2,1)S(1)}, bf16[74,8,128]{2,1,0:T(8,128)(2,1)S(1)}, u32[]{:S(2)}, u32[]{:S(2)}) collective-permute-start(bf16[74,8,128]{2,1,0:T(8,128)(2,1)S(1)} %pad_maximum_fusion.9), channel_id=1, source_target_pairs={{0,12},{4,0},{8,4},{12,8},{1,13},{5,1},{9,5},{13,9},{2,14},{6,2},{... | collective-permute-start | bytes 454664 | tf_op jit(solution)/shard_map/ppermute | solution.py:219
  63.4 0.3 collective-permute-start.7
  63.6 1.6 %collective-permute-start.9 = (bf16[8,8,128]{2,1,0:T(8,128)(2,1)S(1)}, bf16[8,8,128]{2,1,0:T(8,128)(2,1)S(1)}, u32[]{:S(2)}, u32[]{:S(2)}) collective-permute-start(bf16[8,8,128]{2,1,0:T(8,128)(2,1)S(1)} %get-tuple-element.46), channel_id=1, source_target_pairs={{0,8},{4,12},{8,0},{12,4},{1,9},{5,13},{9,1},{13,5},{2,10},{6,14},... | collective-permute-start | bytes 49160 | tf_op jit(solution)/shard_map/ppermute | solution.py:219
  65.2 0.9 collective-permute-done.8
  66.1 2.7 %collective-permute-done.7 = bf16[74,8,128]{2,1,0:T(8,128)(2,1)S(1)} collective-permute-done((bf16[74,8,128]{2,1,0:T(8,128)(2,1)S(1)}, bf16[74,8,128]{2,1,0:T(8,128)(2,1)S(1)}, u32[]{:S(2)}, u32[]{:S(2)}) %collective-permute-start.7) | collective-permute-done | bytes 151584 | tf_op jit(solution)/shard_map/ppermute | solution.py:219
  69.0 0.2 fusion.19
  69.3 1.1 %collective-permute-start.11 = (bf16[3,17,8,128]{3,2,0,1:T(8,128)(2,1)S(1)}, bf16[3,17,8,128]{3,2,0,1:T(8,128)(2,1)S(1)}, u32[]{:S(2)}, u32[]{:S(2)}) collective-permute-start(bf16[3,17,8,128]{3,2,0,1:T(8,128)(2,1)S(1)} %pad_maximum_fusion.16), channel_id=1, source_target_pairs={{0,224},{32,0},{64,32},{96,64},{128,96},{160,128},{192,160},{224,1... | collective-permute-start | bytes 313352 | tf_op jit(solution)/shard_map/ppermute | solution.py:219
  70.4 0.5 collective-permute-start.10
  71.0 2.2 %collective-permute-done.11 = bf16[3,17,8,128]{3,2,0,1:T(8,128)(2,1)S(1)} collective-permute-done((bf16[3,17,8,128]{3,2,0,1:T(8,128)(2,1)S(1)}, bf16[3,17,8,128]{3,2,0,1:T(8,128)(2,1)S(1)}, u32[]{:S(2)}, u32[]{:S(2)}) %collective-permute-start.11) | collective-permute-done | bytes 104480 | tf_op jit(solution)/shard_map/ppermute | solution.py:219
  73.2 2.0 %collective-permute-done.10 = bf16[3,17,8,128]{3,2,0,1:T(8,128)(2,1)S(1)} collective-permute-done((bf16[3,17,8,128]{3,2,0,1:T(8,128)(2,1)S(1)}, bf16[3,17,8,128]{3,2,0,1:T(8,128)(2,1)S(1)}, u32[]{:S(2)}, u32[]{:S(2)}) %collective-permute-start.10) | collective-permute-done | bytes 104480 | tf_op jit(solution)/shard_map/ppermute | solution.py:219
  75.4 0.2 copy.57
  75.7 21.8 %all_to_all.10 = bf16[8,392,128]{2,1,0:T(8,128)(2,1)S(1)} all-to-all(bf16[8,392,128]{2,1,0:T(8,128)(2,1)S(1)} %fusion.4), channel_id=1, replica_groups=mesh['z'=8,'yh'=2,'x'=4,'yl'=2,'core'=2] {'yh','yl','core'}, dimensions={0} | all-to-all | bytes 1605632 | tf_op jit(solution)/shard_map/all_to_all | solution.py:209
  97.7 2.0 %collective-permute-start.13 = (bf16[1,1024]{1,0:T(2,128)(2,1)S(1)}, bf16[1,1024]{1,0:T(2,128)(2,1)S(1)}, u32[]{:S(2)}, u32[]{:S(2)}) collective-permute-start(bf16[1,1024]{1,0:T(2,128)(2,1)S(1)} %get-tuple-element.51), channel_id=1, source_target_pairs={{0,160},{32,192},{64,224},{96,0},{128,32},{160,64},{192,96},{224,1... | collective-permute-start | bytes 6152 | tf_op jit(solution)/shard_map/ppermute | solution.py:219
  99.7 1.4 %collective-permute-start.12 = (bf16[1,1024]{1,0:T(2,128)(2,1)S(1)}, bf16[1,1024]{1,0:T(2,128)(2,1)S(1)}, u32[]{:S(2)}, u32[]{:S(2)}) collective-permute-start(bf16[1,1024]{1,0:T(2,128)(2,1)S(1)} %get-tuple-element.50), channel_id=1, source_target_pairs={{0,96},{32,128},{64,160},{96,192},{128,224},{160,0},{192,32},{224,... | collective-permute-start | bytes 6152 | tf_op jit(solution)/shard_map/ppermute | solution.py:219
  101.1 0.2 fusion.26
  101.4 0.2 reshape.169
  101.6 0.3 copy.60
  102.0 1.0 reshape.170
  103.0 0.3 copy.61
  103.3 1.0 reshape.171
  104.3 0.3 copy.62
  104.7 1.0 reshape.172
  105.7 0.6 fusion.29
  (75 shorter events, 2.0 us)
Async XLA Ops:
  0.6 11.1 %copy-start.2 = (s32[8,8,4]{1,2,0:T(4,128)S(1)}, s32[8,8,4]{1,2,0:T(4,128)}, u32[]{:S(2)}) copy-start(s32[8,8,4]{1,2,0:T(4,128)} %param.13) | copy-start | bytes 3076
  0.6 11.4 %copy-start = (bf16[8,8,4,512]{3,2,1,0:T(4,128)(2,1)S(1)}, bf16[8,8,4,512]{3,2,1,0:T(4,128)(2,1)}, u32[]{:S(2)}) copy-start(bf16[8,8,4,512]{3,2,1,0:T(4,128)(2,1)} %param.10) | copy-start | bytes 786436
  0.7 11.7 %copy-start.1 = (bf16[8,8,4,512]{3,2,1,0:T(4,128)(2,1)S(1)}, bf16[8,8,4,512]{3,2,1,0:T(4,128)(2,1)}, u32[]{:S(2)}) copy-start(bf16[8,8,4,512]{3,2,1,0:T(4,128)(2,1)} %param.7) | copy-start | bytes 786436
  1.7 11.8 %collective-permute-start.1 = (bf16[8,1,128]{2,0,1:T(8,128)(2,1)S(1)}, bf16[8,1,128]{2,0,1:T(8,128)(2,1)S(1)}, u32[]{:S(2)}, u32[]{:S(2)}) collective-permute-start(bf16[8,1,128]{2,0,1:T(8,128)(2,1)S(1)} %bitcast.140), channel_id=1, source_target_pairs={{0,96},{32,128},{64,160},{96,192},{128,224},{160,0},{192,32},{224,... | collective-permute-start | bytes 6152 | tf_op jit(solution)/shard_map/ppermute | solution.py:219
  7.0 6.6 %collective-permute-start = (bf16[8,1,128]{2,0,1:T(8,128)(2,1)S(1)}, bf16[8,1,128]{2,0,1:T(8,128)(2,1)S(1)}, u32[]{:S(2)}, u32[]{:S(2)}) collective-permute-start(bf16[8,1,128]{2,0,1:T(8,128)(2,1)S(1)} %bitcast.141), channel_id=1, source_target_pairs={{0,160},{32,192},{64,224},{96,0},{128,32},{160,64},{192,96},{224,1... | collective-permute-start | bytes 6152 | tf_op jit(solution)/shard_map/ppermute | solution.py:219
  14.8 20.7 %all-to-all-start = ((bf16[8,520,128]{2,1,0:T(8,128)(2,1)}), bf16[8,520,128]{2,1,0:T(8,128)(2,1)S(1)}, u32[]{:S(2)}, u32[]{:S(2)}) async-start(bf16[8,520,128]{2,1,0:T(8,128)(2,1)} %copy.45), calls=%async_computation | async-start | bytes 2129920 | tf_op jit(solution)/shard_map/all_to_all | solution.py:209
  36.0 5.3 %collective-permute-start.3 = (bf16[3,17,8,128]{3,2,0,1:T(8,128)(2,1)S(1)}, bf16[3,17,8,128]{3,2,0,1:T(8,128)(2,1)S(1)}, u32[]{:S(2)}, u32[]{:S(2)}) collective-permute-start(bf16[3,17,8,128]{3,2,0,1:T(8,128)(2,1)S(1)} %get-tuple-element.52), channel_id=1, source_target_pairs={{0,224},{32,0},{64,32},{96,64},{128,96},{160,128},{192,160},{224,1... | collective-permute-start | bytes 313352 | tf_op jit(solution)/shard_map/ppermute | solution.py:219
  38.6 4.7 %collective-permute-start.2 = (bf16[3,17,8,128]{3,2,0,1:T(8,128)(2,1)S(1)}, bf16[3,17,8,128]{3,2,0,1:T(8,128)(2,1)S(1)}, u32[]{:S(2)}, u32[]{:S(2)}) collective-permute-start(bf16[3,17,8,128]{3,2,0,1:T(8,128)(2,1)S(1)} %get-tuple-element.53), channel_id=1, source_target_pairs={{0,32},{32,64},{64,96},{96,128},{128,160},{160,192},{192,224},{224... | collective-permute-start | bytes 313352 | tf_op jit(solution)/shard_map/ppermute | solution.py:219
  43.6 5.3 %collective-permute-start.4 = (bf16[74,8,128]{2,1,0:T(8,128)(2,1)S(1)}, bf16[74,8,128]{2,1,0:T(8,128)(2,1)S(1)}, u32[]{:S(2)}, u32[]{:S(2)}) collective-permute-start(bf16[74,8,128]{2,1,0:T(8,128)(2,1)S(1)} %get-tuple-element.48), channel_id=1, source_target_pairs={{0,4},{4,8},{8,12},{12,0},{1,5},{5,9},{9,13},{13,1},{2,6},{6,10},{... | collective-permute-start | bytes 454664 | tf_op jit(solution)/shard_map/ppermute | solution.py:219
  44.9 4.1 %collective-permute-start.5 = (bf16[74,8,128]{2,1,0:T(8,128)(2,1)S(1)}, bf16[74,8,128]{2,1,0:T(8,128)(2,1)S(1)}, u32[]{:S(2)}, u32[]{:S(2)}) collective-permute-start(bf16[74,8,128]{2,1,0:T(8,128)(2,1)S(1)} %get-tuple-element.49), channel_id=1, source_target_pairs={{0,12},{4,0},{8,4},{12,8},{1,13},{5,1},{9,5},{13,9},{2,14},{6,2},{... | collective-permute-start | bytes 454664 | tf_op jit(solution)/shard_map/ppermute | solution.py:219
  46.4 4.2 %collective-permute-start.6 = (bf16[8,8,128]{2,1,0:T(8,128)(2,1)S(1)}, bf16[8,8,128]{2,1,0:T(8,128)(2,1)S(1)}, u32[]{:S(2)}, u32[]{:S(2)}) collective-permute-start(bf16[8,8,128]{2,1,0:T(8,128)(2,1)S(1)} %pad_maximum_fusion.17), channel_id=1, source_target_pairs={{0,8},{4,12},{8,0},{12,4},{1,9},{5,13},{9,1},{13,5},{2,10},{6,14},... | collective-permute-start | bytes 49160 | tf_op jit(solution)/shard_map/ppermute | solution.py:219
  62.0 4.1 %collective-permute-start.8 = (bf16[74,8,128]{2,1,0:T(8,128)(2,1)S(1)}, bf16[74,8,128]{2,1,0:T(8,128)(2,1)S(1)}, u32[]{:S(2)}, u32[]{:S(2)}) collective-permute-start(bf16[74,8,128]{2,1,0:T(8,128)(2,1)S(1)} %pad_maximum_fusion.9), channel_id=1, source_target_pairs={{0,12},{4,0},{8,4},{12,8},{1,13},{5,1},{9,5},{13,9},{2,14},{6,2},{... | collective-permute-start | bytes 454664 | tf_op jit(solution)/shard_map/ppermute | solution.py:219
  63.4 5.5 %collective-permute-start.7 = (bf16[74,8,128]{2,1,0:T(8,128)(2,1)S(1)}, bf16[74,8,128]{2,1,0:T(8,128)(2,1)S(1)}, u32[]{:S(2)}, u32[]{:S(2)}) collective-permute-start(bf16[74,8,128]{2,1,0:T(8,128)(2,1)S(1)} %pad_maximum_fusion.8), channel_id=1, source_target_pairs={{0,4},{4,8},{8,12},{12,0},{1,5},{5,9},{9,13},{13,1},{2,6},{6,10},{... | collective-permute-start | bytes 454664 | tf_op jit(solution)/shard_map/ppermute | solution.py:219
  63.6 5.3 %collective-permute-start.9 = (bf16[8,8,128]{2,1,0:T(8,128)(2,1)S(1)}, bf16[8,8,128]{2,1,0:T(8,128)(2,1)S(1)}, u32[]{:S(2)}, u32[]{:S(2)}) collective-permute-start(bf16[8,8,128]{2,1,0:T(8,128)(2,1)S(1)} %get-tuple-element.46), channel_id=1, source_target_pairs={{0,8},{4,12},{8,0},{12,4},{1,9},{5,13},{9,1},{13,5},{2,10},{6,14},... | collective-permute-start | bytes 49160 | tf_op jit(solution)/shard_map/ppermute | solution.py:219
  69.3 3.9 %collective-permute-start.11 = (bf16[3,17,8,128]{3,2,0,1:T(8,128)(2,1)S(1)}, bf16[3,17,8,128]{3,2,0,1:T(8,128)(2,1)S(1)}, u32[]{:S(2)}, u32[]{:S(2)}) collective-permute-start(bf16[3,17,8,128]{3,2,0,1:T(8,128)(2,1)S(1)} %pad_maximum_fusion.16), channel_id=1, source_target_pairs={{0,224},{32,0},{64,32},{96,64},{128,96},{160,128},{192,160},{224,1... | collective-permute-start | bytes 313352 | tf_op jit(solution)/shard_map/ppermute | solution.py:219
  70.4 4.8 %collective-permute-start.10 = (bf16[3,17,8,128]{3,2,0,1:T(8,128)(2,1)S(1)}, bf16[3,17,8,128]{3,2,0,1:T(8,128)(2,1)S(1)}, u32[]{:S(2)}, u32[]{:S(2)}) collective-permute-start(bf16[3,17,8,128]{3,2,0,1:T(8,128)(2,1)S(1)} %pad_maximum_fusion.15), channel_id=1, source_target_pairs={{0,32},{32,64},{64,96},{96,128},{128,160},{160,192},{192,224},{224... | collective-permute-start | bytes 313352 | tf_op jit(solution)/shard_map/ppermute | solution.py:219
  97.7 7.9 %collective-permute-start.13 = (bf16[1,1024]{1,0:T(2,128)(2,1)S(1)}, bf16[1,1024]{1,0:T(2,128)(2,1)S(1)}, u32[]{:S(2)}, u32[]{:S(2)}) collective-permute-start(bf16[1,1024]{1,0:T(2,128)(2,1)S(1)} %get-tuple-element.51), channel_id=1, source_target_pairs={{0,160},{32,192},{64,224},{96,0},{128,32},{160,64},{192,96},{224,1... | collective-permute-start | bytes 6152 | tf_op jit(solution)/shard_map/ppermute | solution.py:219
  99.7 6.0 %collective-permute-start.12 = (bf16[1,1024]{1,0:T(2,128)(2,1)S(1)}, bf16[1,1024]{1,0:T(2,128)(2,1)S(1)}, u32[]{:S(2)}, u32[]{:S(2)}) collective-permute-start(bf16[1,1024]{1,0:T(2,128)(2,1)S(1)} %get-tuple-element.50), channel_id=1, source_target_pairs={{0,96},{32,128},{64,160},{96,192},{128,224},{160,0},{192,32},{224,... | collective-permute-start | bytes 6152 | tf_op jit(solution)/shard_map/ppermute | solution.py:219
